TPU v7x, 128 devices: a whole 4x4x4 slice. The times are simulated.
128 devices in a mesh: row: 16 (over x, z), col: 8 (over y, core).
Axes of the slice: x: 4, y: 4, z: 4, core: 2. Of those that a mesh axis runs over, the one named last changes fastest.
Arguments:
- kernel_tiles: float32 [1, 16, 2, 8, 1024, 1024], P(None, 'row', None, 'col'), may hold values from 0 to 2.5, as said below
- profile: int32 [2, 16], replicated, may hold values from 0 to 15, as said below
Outputs:
- factored: float32 [1, 16, 2, 8, 1024, 1024], P(None, 'row', None, 'col')
Inputs may be any that keep to these rules, and one draw needn't show every extreme that they name: profile[0] never falls along the tile rows; profile[0, i] >= i - 9, and profile[0, i] = 0 for i <= 9; profile[1, i] is the last j with profile[0, j] <= i. `kernel_tiles`: symmetric; every tile outside the pattern is zero; the matrix restricted to the pattern is positive definite.
All inputs are finite; a program needn't handle non-finite values.
Results may differ from a plain program's by a relative error of at most 0.0001.
Values sent between devices are 32-bit elements; how exact they have to be, the bound alone decides.
A program may use at most 256 MiB of HBM per device.

v0:
```python
import jax
import jax.numpy as jnp
from jax import lax
from jax.sharding import PartitionSpec as P

STEPS = 2


def from_root(value, axis, root):
    mine = lax.axis_index(axis) == root
    return lax.psum(jnp.where(mine, value, jnp.zeros_like(value)), axis)


def solve_right(block_tile, lower_factor):
    return lax.linalg.triangular_solve(
        lower_factor, block_tile, left_side=False, lower=True, transpose_a=True
    )


def zero_like(block_tile, lower_factor):
    return jnp.zeros_like(block_tile)


def zero_factor(block_tile):
    return jnp.zeros_like(block_tile)


def subtract_outer(target, left_tile, right_tile):
    product = lax.dot_general(
        left_tile,
        right_tile,
        (((1,), (1,)), ((), ())),
        precision=lax.Precision.HIGHEST,
        preferred_element_type=jnp.float32,
    )
    return target - product


def keep_target(target, left_tile, right_tile):
    return target


def on_device(kernel_tiles, profile):
    rows_here = kernel_tiles.shape[0]
    cols_here = kernel_tiles.shape[2]
    order = kernel_tiles.shape[-1]
    blocks = kernel_tiles.reshape(rows_here, cols_here, order, order)
    row_count = lax.axis_size("row")
    col_count = lax.axis_size("col")
    row_index = lax.axis_index("row")
    col_index = lax.axis_index("col")
    global_row = jnp.arange(rows_here, dtype=jnp.int32) * row_count + row_index
    global_col = jnp.arange(cols_here, dtype=jnp.int32) * col_count + col_index
    first_col = profile[0]
    last_col = profile[1]
    row_first = first_col[global_row]
    row_last = last_col[global_row]
    col_first = first_col[global_col]
    in_pattern = jnp.where(
        global_row[:, None] >= global_col[None, :],
        row_first[:, None] <= global_col[None, :],
        global_col[None, :] <= row_last[:, None],
    )
    blocks = jnp.where(in_pattern[:, :, None, None], blocks, jnp.float32(0.0))
    for step in range(STEPS):
        owner_row = step % row_count
        owner_col = step % col_count
        local_row = step // row_count
        local_col = step // col_count
        live_row = (global_row > step) & (row_first <= step)
        live_col = (global_col > step) & (col_first <= step)
        diag_tile = from_root(blocks[local_row, local_col], "row", owner_row)
        diag_factor = lax.cond(col_index == owner_col, jnp.linalg.cholesky, zero_factor, diag_tile)
        solved = jnp.stack(
            [
                lax.cond(
                    live_row[0] & (col_index == owner_col),
                    solve_right,
                    zero_like,
                    blocks[0, local_col],
                    diag_factor,
                )
            ]
        )
        panel_here = from_root(solved, "col", owner_col)
        copies = []
        for slot in range(cols_here):
            wanted = global_col[slot]
            source = lax.dynamic_index_in_dim(panel_here, wanted // row_count, 0, keepdims=False)
            copies.append(from_root(source, "row", wanted % row_count))
        across = jnp.stack(copies)
        updated = []
        for col_slot in range(cols_here):
            active = live_row[0] & live_col[col_slot]
            target = lax.cond(
                active,
                subtract_outer,
                keep_target,
                blocks[0, col_slot],
                panel_here[0],
                across[col_slot],
            )
            is_col = global_col[col_slot] == step
            target = jnp.where(is_col & (global_row[0] > step), panel_here[0], target)
            target = jnp.where(is_col & (global_row[0] == step), diag_factor, target)
            target = jnp.where(
                (global_row[0] == step) & (global_col[col_slot] > step), jnp.float32(0.0), target
            )
            updated.append(target)
        updated_rows = [jnp.stack(updated)]
        blocks = jnp.stack(updated_rows)
    return blocks.reshape(kernel_tiles.shape)


def solution(mesh):
    placed = (P(None, "row", None, "col", None, None), P())
    return jax.shard_map(
        on_device,
        mesh=mesh,
        in_specs=placed,
        out_specs=P(None, "row", None, "col", None, None),
        check_vma=False,
    )
```

profile of v0, /device:TPU:76, one launch (start us, length us, event | category | flops | bytes accessed | tf_op | source)
XLA Modules:
  0.0 1503.5 jit_solution(11153229942905519610)
XLA Ops:
  6.5 0.8 slice_bitcast_fusion.36
  7.3 0.7 fusion.146
  8.6 1.3 compare_select_fusion.1
  9.9 4.4 bitcast_select_fusion
  14.4 3.4 copy-done.3
  17.8 2.4 broadcast_select_fusion.7
  20.9 8.3 slice_bitcast_fusion.34
  29.2 94.6 %all-reduce.10.cloned.1.call-done = f32[1024,1024]{1,0:T(8,128)} async-done(((f32[1024,1024]{1,0:T(8,128)}), f32[1024,1024]{1,0:T(8,128)}) %all-reduce.10.cloned.1.call-update) | async-done | bytes 4194320 | tf_op jit(solution)/shard_map/psum | solution.py:11
  123.8 5.4 conditional.8
  123.8 2.5 broadcast.349
  129.2 14.9 conditional.9
  129.2 2.5 broadcast.352.clone
  144.1 2.8 broadcast_select_fusion.6
  151.6 423.2 %all-reduce.12.cloned.1.call-done = f32[1024,1024]{1,0:T(8,128)} async-done(((f32[1024,1024]{1,0:T(8,128)}), f32[1024,1024]{1,0:T(8,128)}) %all-reduce.12.cloned.1.call-update) | async-done | bytes 4194320 | tf_op jit(solution)/shard_map/psum | solution.py:11
  574.9 7.0 broadcast_select_fusion.5
  587.0 136.8 %all-reduce.20.cloned.1.call-done = (f32[1024,1024]{1,0:T(8,128)}, f32[1024,1024]{1,0:T(8,128)}) async-done(((f32[1024,1024]{1,0:T(8,128)}, f32[1024,1024]{1,0:T(8,128)}), (f32[1024,1024]{1,0:T(8,128)}, f32[1024,1024]{1,0:T(8,128)})) %all-reduce.20.cloned.1.call-update) | async-done | bytes 8388624 | tf_op jit(solution)/shard_map/psum | solution.py:11
  724.0 10.4 select_bitcast_fusion.17
  734.5 3.0 maximum_bitcast_fusion
  737.5 3.4 copy-done.2
  740.9 2.4 broadcast_select_fusion.3
  744.0 8.3 slice_bitcast_fusion.32
  752.3 126.7 %all-reduce.14.cloned.1.call-done = f32[1024,1024]{1,0:T(8,128)} async-done(((f32[1024,1024]{1,0:T(8,128)}), f32[1024,1024]{1,0:T(8,128)}) %all-reduce.14.cloned.1.call-update) | async-done | bytes 4194320 | tf_op jit(solution)/shard_map/psum | solution.py:11
  879.0 5.6 conditional.12
  879.0 2.5 broadcast.356
  884.6 14.6 conditional.13
  884.6 2.5 broadcast.357.clone
  899.2 2.8 broadcast_select_fusion.2
  902.1 427.7 %all-reduce.16.cloned.1.call-done = f32[1024,1024]{1,0:T(8,128)} async-done(((f32[1024,1024]{1,0:T(8,128)}), f32[1024,1024]{1,0:T(8,128)}) %all-reduce.16.cloned.1.call-update) | async-done | bytes 4194320 | tf_op jit(solution)/shard_map/psum | solution.py:11
  1329.7 7.0 broadcast_select_fusion.1
  1340.6 138.1 %all-reduce.18.cloned.1.call-done = (f32[1024,1024]{1,0:T(8,128)}, f32[1024,1024]{1,0:T(8,128)}) async-done(((f32[1024,1024]{1,0:T(8,128)}, f32[1024,1024]{1,0:T(8,128)}), (f32[1024,1024]{1,0:T(8,128)}, f32[1024,1024]{1,0:T(8,128)})) %all-reduce.18.cloned.1.call-update) | async-done | bytes 8388624 | tf_op jit(solution)/shard_map/psum | solution.py:11
  1479.0 10.4 select_bitcast_fusion.15
  1489.4 6.8 maximum_bitcast_fusion.1
  (26 shorter events, 3.4 us)
Async XLA Ops:
  6.5 117.3 %all-reduce.10.cloned.1.call-start = ((), (), s32[]{:S(2)}) async-start(), calls=%async_computation | async-start | bytes 8388608 | tf_op jit(solution)/shard_map/psum | solution.py:11
  14.4 3.4 copy-start.3
  20.2 554.7 %all-reduce.12.cloned.1.call-start = ((), (), s32[]{:S(2)}) async-start(), calls=%async_computation.1 | async-start | bytes 8388608 | tf_op jit(solution)/shard_map/psum | solution.py:11
  147.0 576.9 %all-reduce.20.cloned.1.call-start = ((), (), s32[]{:S(2)}) async-start(), calls=%async_computation.5 | async-start | bytes 16777216 | tf_op jit(solution)/shard_map/psum | solution.py:11
  581.9 297.1 %all-reduce.14.cloned.1.call-start = ((), (), s32[]{:S(2)}) async-start(), calls=%async_computation.2 | async-start | bytes 8388608 | tf_op jit(solution)/shard_map/psum | solution.py:11
  737.5 3.4 copy-start.2
  743.3 586.4 %all-reduce.16.cloned.1.call-start = ((), (), s32[]{:S(2)}) async-start(), calls=%async_computation.3 | async-start | bytes 8388608 | tf_op jit(solution)/shard_map/psum | solution.py:11
  902.0 576.7 %all-reduce.18.cloned.1.call-start = ((), (), s32[]{:S(2)}) async-start(), calls=%async_computation.4 | async-start | bytes 16777216 | tf_op jit(solution)/shard_map/psum | solution.py:11
Sparse Core Ops, SparseCore 0:
  20.3 103.4 all-reduce.9
  147.1 427.7 all-reduce.11
  582.0 141.7 all-reduce.19
  743.4 135.5 all-reduce.13
  902.2 427.5 all-reduce.15
  1336.9 141.7 all-reduce.17
where the time goes:
time: 1530 us; the launch traced here: 1500 us
  waiting for transfers between devices  1350 us (88%)
  other arithmetic  61.4 us (4%)
  local copies, waits for them, and re-layouts  36.8 us (2%)
  loops' own time  30.9 us (2%)
  between operations  27 us (2%)
    psum x6, waiting for transfers between devices, from_root(): return lax.psum(jnp.where(mine, value, jnp.zeros_like(value)), axis)  1350 us
  transfers between devices with their start and end apart: 6, of which 6 were waited for; matrix products, arithmetic and copies ran while one was open for 1% of the time, Pallas kernels for 0%

commit v1 on v0

v1 whole, which is shorter than its diff:
```python
import jax
import jax.numpy as jnp
from jax import lax
from jax.experimental import pallas as pl
from jax.experimental.pallas import tpu as pltpu
from jax.sharding import PartitionSpec as P

F32 = jnp.float32
BF16 = jnp.bfloat16
TILE = 1024
HALF = 128
BLK = 256
NB = 8


def dot_nt(a, b):
    return lax.dot_general(
        a, b, (((1,), (1,)), ((), ())),
        precision=lax.Precision.HIGHEST, preferred_element_type=F32,
    )


def dot_nn(a, b):
    return lax.dot_general(
        a, b, (((1,), (0,)), ((), ())),
        precision=lax.Precision.HIGHEST, preferred_element_type=F32,
    )


def split3(x):
    high = x.astype(BF16).astype(F32)
    rest = x - high
    mid = rest.astype(BF16).astype(F32)
    return high, mid, rest - mid


def split2(x):
    high = x.astype(BF16)
    return high, (x - high.astype(F32)).astype(BF16)


def dot3(a, b, b_dim):
    dims = (((1,), (b_dim,)), ((), ()))

    def one(p, q):
        return lax.dot_general(p, q, dims, preferred_element_type=F32)

    return one(a[0], b[0]) + one(a[0], b[1]) + one(a[1], b[0])


def leaf(work):
    sub = lax.broadcasted_iota(jnp.int32, (8, 2 * HALF), 0)
    for o in range(0, HALF, 8):
        rows = [jnp.broadcast_to(work[o + p:o + p + 1, :], (8, 2 * HALF)) for p in range(8)]
        a = [
            [jnp.broadcast_to(rows[p][:, o + q:o + q + 1], (8, HALF)) for q in range(p + 1)]
            for p in range(8)
        ]
        low = [[None] * 8 for _ in range(8)]
        done = []
        for q in range(8):
            s = lax.rsqrt(a[q][q])
            for p in range(q + 1, 8):
                low[p][q] = a[p][q] * s
            for p in range(q + 1, 8):
                for t in range(q + 1, p + 1):
                    a[p][t] = a[p][t] - low[p][q] * low[t][q]
            acc = rows[q]
            for t in range(q):
                acc = acc - jnp.concatenate([low[q][t], low[q][t]], axis=1) * done[t]
            done.append(acc * jnp.concatenate([s, s], axis=1))
        u = done[0]
        for q in range(1, 8):
            u = jnp.where(sub == q, done[q], u)
        work[o:o + 8, :] = u
        if o + 8 < HALF:
            h, m, l = split3(u)
            left = jnp.concatenate([v[:, :HALF] for v in (h, h, m, h, l, m)], axis=0).astype(BF16)
            right = jnp.concatenate([h, m, h, l, h, m], axis=0).astype(BF16)
            update = lax.dot_general(
                left, right, (((0,), (0,)), ((), ())), preferred_element_type=F32
            )
            work[o + 8:, :] = work[o + 8:, :] - update[o + 8:, :]


def leaf_factor(work, block):
    ri = lax.broadcasted_iota(jnp.int32, (HALF, HALF), 0)
    ci = lax.broadcasted_iota(jnp.int32, (HALF, HALF), 1)
    work[:, :HALF] = block
    work[:, HALF:] = jnp.where(ri == ci, 1.0, 0.0).astype(F32)
    leaf(work)
    upper = jnp.where(ci >= ri, work[:, :HALF], 0.0)
    inverse = jnp.where(ci <= ri, work[:, HALF:], 0.0)
    return upper, inverse


def block_factor(k, s, work, linv):
    here = pl.ds(pl.multiple_of(k * BLK, BLK), BLK)
    block = s[k, here, :]
    u1, inv1 = leaf_factor(work, block[:HALF, :HALF])
    l21 = dot_nt(block[HALF:, :HALF], inv1)
    u2, inv2 = leaf_factor(work, block[HALF:, HALF:] - dot_nt(l21, l21))
    inv21 = -dot_nn(inv2, dot_nn(l21, inv1))
    zero = jnp.zeros((HALF, HALF), F32)
    linv[k, :HALF, :HALF] = inv1
    linv[k, :HALF, HALF:] = zero
    linv[k, HALF:, :HALF] = inv21
    linv[k, HALF:, HALF:] = inv2
    s[k, here, :] = jnp.concatenate(
        [jnp.concatenate([u1.T, zero], axis=1), jnp.concatenate([l21, u2.T], axis=1)], axis=0
    )


def rows_of(i):
    return pl.ds(pl.multiple_of(i * BLK, BLK), BLK)


def panel_step(k, s, linv):
    @pl.loop(k + 1, NB)
    def _(i):
        s[k, rows_of(i), :] = dot_nt(s[k, rows_of(i), :], linv[k])


def trailing_step(k, s):
    @pl.loop(k + 1, NB)
    def _(j):
        @pl.loop(j, NB)
        def _(i):
            s[j, rows_of(i), :] = s[j, rows_of(i), :] - dot_nt(s[k, rows_of(i), :], s[k, rows_of(j), :])


def factor_kernel(a_ref, l_ref, linv_ref, s, work, sem):
    loads = []
    for j in range(NB):
        cols = pl.ds((j % 4) * BLK, BLK)
        if j < 4:
            loads.append(pltpu.make_async_copy(a_ref.at[0, :, cols], s.at[j, pl.ds(0, TILE)], sem.at[j, 0]))
        low = a_ref.at[1, :, cols] if j < 4 else a_ref.at[2, :, cols]
        loads.append(pltpu.make_async_copy(low, s.at[j, pl.ds(TILE, TILE)], sem.at[j, 1]))
    for c in loads:
        c.start()
    for c in loads:
        c.wait()

    @pl.loop(0, NB)
    def _(k):
        block_factor(k, s, work, linv_ref)
        panel_step(k, s, linv_ref)
        trailing_step(k, s)

    out = [pltpu.make_async_copy(s.at[j], l_ref.at[j], sem.at[j, 0]) for j in range(NB)]
    for c in out:
        c.start()
    for c in out:
        c.wait()


def factor(a):
    return pl.pallas_call(
        factor_kernel,
        out_shape=(
            jax.ShapeDtypeStruct((NB, 2 * TILE, BLK), F32),
            jax.ShapeDtypeStruct((NB, BLK, BLK), F32),
        ),
        in_specs=[pl.BlockSpec(memory_space=pl.ANY)],
        out_specs=(pl.BlockSpec(memory_space=pl.ANY), pl.BlockSpec(memory_space=pltpu.VMEM)),
        scratch_shapes=[
            pltpu.VMEM((NB, 2 * TILE, BLK), F32),
            pltpu.VMEM((HALF, 2 * HALF), F32),
            pltpu.SemaphoreType.DMA((NB, 2)),
        ],
        compiler_params=pltpu.CompilerParams(vmem_limit_bytes=50 * 2**20),
        name="factor",
    )(a)


def update_kernel(tiles, wi_ref, wj_ref, w10_ref, l_ref, linv_ref, out, w, v, v10, lbuf, t, sem, lsem, osem):
    r = lax.axis_index("row")
    c = lax.axis_index("col")
    live = r < 11
    full = (r >= 2) & live
    slot_a = jnp.where(c >= 2, 0, 1)
    slot_b = 1 - slot_a

    @pl.when(live)
    def _():
        loads = []
        for j in range(NB):
            cols = pl.ds((j % 4) * BLK, BLK)
            loads.append(pltpu.make_async_copy(wi_ref.at[j // 4, :, cols], w.at[j], sem.at[j]))
            loads.append(pltpu.make_async_copy(
                wj_ref.at[j // 4, pl.ds((j % 4) * BLK, BLK), :], v.at[j], sem.at[NB + j]))
        loads.append(pltpu.make_async_copy(w10_ref, v10, sem.at[2 * NB]))
        loads.append(pltpu.make_async_copy(tiles.at[slot_a], t.at[0], sem.at[2 * NB + 1]))
        loads.append(pltpu.make_async_copy(tiles.at[slot_b], t.at[1], sem.at[2 * NB + 2]))
        for x in loads:
            x.start()
        for x in loads:
            x.wait()

        @pl.loop(0, NB)
        def _(k):
            ld = pltpu.make_async_copy(l_ref.at[k], lbuf, lsem)
            ld.start()
            inv = split2(linv_ref[k])
            ld.wait()
            for rc in range(4):
                rows = pl.ds(rc * BLK, BLK)
                p = dot3(split2(w[k, rows, :]), inv, 1)
                w[k, rows, :] = p
                ps = split2(p)

                @pl.loop(k + 1, NB)
                def _(j):
                    w[j, rows, :] = w[j, rows, :] - dot3(ps, split2(lbuf[rows_of(j), :]), 1)

            @pl.when(full)
            def _():
                v[k] = dot3(inv, split2(v[k]), 0)
                vs = split2(v[k])

                @pl.loop(k + 1, NB)
                def _(j):
                    v[j] = v[j] - dot3(split2(lbuf[rows_of(j), :]), vs, 0)

                for rc in range(4):
                    rows = pl.ds(rc * BLK, BLK)
                    t[0, rows, :] = t[0, rows, :] - dot3(split2(w[k, rows, :]), vs, 0)

            @pl.when(full & (c == 2) & (k >= 4))
            def _():
                at = pl.ds(pl.multiple_of((k - 4) * BLK, BLK), BLK)
                v10[at, :] = dot3(inv, split2(v10[at, :]), 0)
                vs = split2(v10[at, :])

                @pl.loop(k + 1, NB)
                def _(j):
                    to = pl.ds(pl.multiple_of((j - 4) * BLK, BLK), BLK)
                    v10[to, :] = v10[to, :] - dot3(split2(lbuf[rows_of(j), :]), vs, 0)

                for rc in range(4):
                    rows = pl.ds(rc * BLK, BLK)
                    t[1, rows, :] = t[1, rows, :] - dot3(split2(w[k, rows, :]), vs, 0)

    @pl.when(r < 2)
    def _():
        t[0] = jnp.zeros((TILE, TILE), F32)
        t[1] = jnp.zeros((TILE, TILE), F32)

    @pl.when((r < 11) & (c < 2) & (r >= c))
    def _():
        for j in range(4):
            ri = lax.broadcasted_iota(jnp.int32, (TILE, BLK), 0)
            ci = lax.broadcasted_iota(jnp.int32, (TILE, BLK), 1) + j * BLK
            keep = (r > c) | (ri >= ci)
            t[1, :, j * BLK:(j + 1) * BLK] = jnp.where(keep, w[c * 4 + j], 0.0)

    @pl.when(live)
    def _():
        o = [pltpu.make_async_copy(t.at[0], out.at[slot_a], osem.at[0]),
             pltpu.make_async_copy(t.at[1], out.at[slot_b], osem.at[1])]
        for x in o:
            x.start()
        for x in o:
            x.wait()

    @pl.when(r >= 11)
    def _():
        o = [pltpu.make_async_copy(tiles.at[n], out.at[n], osem.at[n]) for n in range(2)]
        for x in o:
            x.start()
        for x in o:
            x.wait()


def update(tiles, wi, wj, w10, l, linv):
    anywhere = pl.BlockSpec(memory_space=pl.ANY)
    return pl.pallas_call(
        update_kernel,
        out_shape=jax.ShapeDtypeStruct((2, TILE, TILE), F32),
        in_specs=[anywhere] * 5 + [pl.BlockSpec(memory_space=pltpu.VMEM)],
        out_specs=anywhere,
        scratch_shapes=[
            pltpu.VMEM((NB, TILE, BLK), F32),
            pltpu.VMEM((NB, BLK, TILE), F32),
            pltpu.VMEM((TILE, TILE), F32),
            pltpu.VMEM((2 * TILE, BLK), F32),
            pltpu.VMEM((2, TILE, TILE), F32),
            pltpu.SemaphoreType.DMA((2 * NB + 3,)),
            pltpu.SemaphoreType.DMA,
            pltpu.SemaphoreType.DMA((2,)),
        ],
        compiler_params=pltpu.CompilerParams(vmem_limit_bytes=58 * 2**20),
        name="update",
    )(tiles, wi, wj, w10, l, linv)


def on_device(kernel_tiles, profile):
    tiles = kernel_tiles.reshape(2, TILE, TILE)
    r = lax.axis_index("row")
    c = lax.axis_index("col")
    zero = jnp.zeros((TILE, TILE), F32)
    a = lax.psum(
        jnp.stack([
            jnp.where((r == 0) & (c == 0), tiles[0], zero),
            jnp.where((r == 1) & (c == 0), tiles[0], zero),
            jnp.where((r == 1) & (c == 1), tiles[0], zero),
        ]), ("row", "col"))
    l, linv = factor(a)
    wi = lax.psum(jnp.stack([jnp.where(c == n, tiles[0], zero) for n in range(2)]), "col")
    mine = jnp.where(c >= 2, tiles[0], tiles[1])
    wj = lax.psum(jnp.stack([jnp.where(r == n, mine, zero) for n in range(2)]
                            + [jnp.where(r == 1, tiles[1], zero)]), "row")
    out = update(tiles, wi, wj[:2], wj[2], l, linv)
    return out.reshape(kernel_tiles.shape)


def solution(mesh):
    placed = (P(None, "row", None, "col", None, None), P())
    return jax.shard_map(
        on_device,
        mesh=mesh,
        in_specs=placed,
        out_specs=P(None, "row", None, "col", None, None),
        check_vma=False,
    )
```

time: 1530 us -> 745 us (0.49)
  the two profiles are of different devices: /device:TPU:76 before, /device:TPU:6 now
where the time goes in v1:
time: 745 us; the launch traced here: 744 us
  Pallas kernels  406 us (54%)
  waiting for transfers between devices  276 us (37%)
  other arithmetic  34.8 us (5%)
  local copies, waits for them, and re-layouts  14.7 us (2%)
  between operations  13.1 us (2%)
    pallas_call x1, Pallas kernels, update(): pl.pallas_call(update_kernel, out_shape=jax.ShapeDtypeStruct((2, TILE, TI...  257 us
    psum x1, waiting for transfers between devices, on_device(): lax.psum(jnp.stack([jnp.where((r == 0) & (c == 0), tiles[0], zero), jnp.w...  152 us
    pallas_call x1, Pallas kernels, factor(): pl.pallas_call(factor_kernel, out_shape=(jax.ShapeDtypeStruct((NB, 2 * TI...  149 us
    psum x1, waiting for transfers between devices, on_device(): lax.psum(jnp.stack([jnp.where(c == n, tiles[0], zero) for n in range(2)])...  92.8 us
    psum x1, waiting for transfers between devices, on_device(): lax.psum(jnp.stack([jnp.where(r == n, mine, zero) for n in range(2)] + [j...  31.7 us
  transfers between devices with their start and end apart: 3, of which 3 were waited for; matrix products, arithmetic and copies ran while one was open for 4% of the time, Pallas kernels for 20%

profile of v1, /device:TPU:6, one launch (start us, length us, event | category | flops | bytes accessed | tf_op | source)
XLA Modules:
  0.0 744.5 jit_solution(14701630117818291203)
XLA Ops:
  6.5 0.0 all-reduce.8.cloned.1.call-start
  6.5 10.3 %select_bitcast_fusion.2 = (f32[1,1024,1024]{2,1,0:T(8,128)S(1)}, f32[1,1024,1024]{2,1,0:T(8,128)}, f32[1,1024,1024]{2,1,0:T(8,128)}, f32[1,1024,1024]{2,1,0:T(8...) fusion(f32[1,1,2,1,1024,1024]{5,4,3,2,1,0:T(8,128)} %param.2, ...), kind=kLoop, calls=%fused_computation.6 | loop fusion | flops 9437184 | bytes 41943048 | tf_op jit(solution)/shard_map/jit(_where)/select_n | solution.py:305
  16.8 4.8 pad_maximum_fusion.1
  21.7 0.0 all-reduce.8.cloned.1.call-update
  21.7 0.0 all-reduce.6.cloned.1.call-start
  21.7 10.6 %pad_maximum_fusion = f32[3,1024,1024]{2,1,0:T(8,128)} fusion(f32[1,1024,1024]{2,1,0:T(8,128)} %get-tuple-element.14, f32[1,1024,1024]{2,1,0:T(8,128)} %get-tuple-element.10, f32[1,1024,1024]{2,1,0:T(8,128)} %get-tuple-element.15), kind=kLoop, calls=%fused_computation | loop fusion | flops 6291456 | bytes 25165824 | tf_op jit(solution)/shard_map/stack | solution.py:312
  32.3 0.0 all-reduce.6.cloned.1.call-update
  32.4 0.0 all-reduce.4.cloned.1.call-start
  32.4 9.1 %pad_maximum_fusion.2 = f32[2,1024,1024]{2,1,0:T(8,128)} fusion(f32[1,1024,1024]{2,1,0:T(8,128)} %get-tuple-element.11, f32[1,1024,1024]{2,1,0:T(8,128)} %get-tuple-element.16), kind=kLoop, calls=%fused_computation.2 | loop fusion | flops 2097152 | bytes 16777216 | tf_op jit(solution)/shard_map/stack | solution.py:310
  41.5 0.0 all-reduce.4.cloned.1.call-update
  41.5 151.6 %all-reduce.8.cloned.1.call-done.a_ref = f32[3,1024,1024]{2,1,0:T(8,128)} async-done(((f32[3,1024,1024]{2,1,0:T(8,128)}), f32[3,1024,1024]{2,1,0:T(8,128)}) %all-reduce.8.cloned.1.call-update) | async-done | bytes 12582928 | tf_op jit(solution)/shard_map/psum | solution.py:303
  193.1 148.7 %factor.1 = (f32[8,2048,256]{2,1,0:T(8,128)}, f32[8,256,256]{2,1,0:T(8,128)S(1)}) custom-call(f32[3,1024,1024]{2,1,0:T(8,128)} %all-reduce.8.cloned.1.call-done.a_ref), custom_call_target="tpu_custom_call" | custom-call | tf_op jit(solution)/shard_map/factor/pallas_call | solution.py:159
  341.8 0.0 copy-start
  341.8 1.3 copy-done
  343.1 31.7 %all-reduce.6.cloned.1.call-done = f32[3,1024,1024]{2,1,0:T(8,128)} async-done(((f32[3,1024,1024]{2,1,0:T(8,128)}), f32[3,1024,1024]{2,1,0:T(8,128)}) %all-reduce.6.cloned.1.call-update) | async-done | bytes 12582928 | tf_op jit(solution)/shard_map/psum | solution.py:312
  374.8 8.4 %slice.24.wj_ref = f32[2,1024,1024]{2,1,0:T(8,128)} slice(f32[3,1024,1024]{2,1,0:T(8,128)} %all-reduce.6.cloned.1.call-done), slice={[0:2], [0:1024], [0:1024]} | slice | bytes 16777216 | tf_op jit(solution)/shard_map/slice | solution.py:314
  383.2 4.9 slice_bitcast_fusion.w10_ref
  388.1 92.8 %all-reduce.4.cloned.1.call-done.wi_ref = f32[2,1024,1024]{2,1,0:T(8,128)} async-done(((f32[2,1024,1024]{2,1,0:T(8,128)}), f32[2,1024,1024]{2,1,0:T(8,128)}) %all-reduce.4.cloned.1.call-update) | async-done | bytes 8388624 | tf_op jit(solution)/shard_map/psum | solution.py:310
  480.9 257.0 %update.1 = f32[2,1024,1024]{2,1,0:T(8,128)} custom-call(f32[2,1024,1024]{2,1,0:T(8,128)} %bitcast.22, f32[2,1024,1024]{2,1,0:T(8,128)} %all-reduce.4.cloned.1.call-done.wi_ref, f32[2,1024,1024]{2,1,0:T(8,128)} %slice.24.wj_ref, f32[1024,1024]{1,0:T(8,128)} %slice_bitcast_fusion.w10_ref, f32[8,2048,256]{2,1,0:T(8,128)} %get-tuple-element.7.l_ref, ...), custom_call_target="tpu_custom_call" | custom-call | tf_op jit(solution)/shard_map/update/pallas_call | solution.py:278
Async XLA Ops:
  6.5 186.5 %all-reduce.8.cloned.1.call-start = ((), (), s32[]{:S(2)}) async-start(), calls=%async_computation.2 | async-start | bytes 25165824 | tf_op jit(solution)/shard_map/psum | solution.py:303
  21.7 353.1 %all-reduce.6.cloned.1.call-start = ((), (), s32[]{:S(2)}) async-start(), calls=%async_computation.1 | async-start | bytes 25165824 | tf_op jit(solution)/shard_map/psum | solution.py:312
  32.4 448.6 %all-reduce.4.cloned.1.call-start = ((), (), s32[]{:S(2)}) async-start(), calls=%async_computation | async-start | bytes 16777216 | tf_op jit(solution)/shard_map/psum | solution.py:310
  341.8 1.3 copy-start
Sparse Core Ops, SparseCore 0:
  21.8 171.2 all-reduce.7
  197.2 177.5 all-reduce.5
  377.2 103.7 all-reduce.3

commit v2 on v1

v2 whole, which is shorter than its diff:
```python
import jax
import jax.numpy as jnp
from jax import lax
from jax.experimental import pallas as pl
from jax.experimental.pallas import tpu as pltpu
from jax.sharding import PartitionSpec as P

F32 = jnp.float32
BF16 = jnp.bfloat16
TILE = 1024
HALF = 128
BLK = 256
NB = 8


def dot_nt(a, b):
    return lax.dot_general(
        a, b, (((1,), (1,)), ((), ())),
        precision=lax.Precision.HIGHEST, preferred_element_type=F32,
    )


def dot_nn(a, b):
    return lax.dot_general(
        a, b, (((1,), (0,)), ((), ())),
        precision=lax.Precision.HIGHEST, preferred_element_type=F32,
    )


def split3(x):
    high = x.astype(BF16).astype(F32)
    rest = x - high
    mid = rest.astype(BF16).astype(F32)
    return high, mid, rest - mid


def split2(x):
    high = x.astype(BF16)
    return high, (x - high.astype(F32)).astype(BF16)


def dot3(a, b, b_dim):
    dims = (((1,), (b_dim,)), ((), ()))

    def one(p, q):
        return lax.dot_general(p, q, dims, preferred_element_type=F32)

    return one(a[0], b[0]) + one(a[0], b[1]) + one(a[1], b[0])


def leaf(work):
    sub = lax.broadcasted_iota(jnp.int32, (8, 2 * HALF), 0)
    for o in range(0, HALF, 8):
        rows = [jnp.broadcast_to(work[o + p:o + p + 1, :], (8, 2 * HALF)) for p in range(8)]
        a = [
            [jnp.broadcast_to(rows[p][:, o + q:o + q + 1], (8, HALF)) for q in range(p + 1)]
            for p in range(8)
        ]
        low = [[None] * 8 for _ in range(8)]
        done = []
        for q in range(8):
            s = lax.rsqrt(a[q][q])
            for p in range(q + 1, 8):
                low[p][q] = a[p][q] * s
            for p in range(q + 1, 8):
                for t in range(q + 1, p + 1):
                    a[p][t] = a[p][t] - low[p][q] * low[t][q]
            acc = rows[q]
            for t in range(q):
                acc = acc - jnp.concatenate([low[q][t], low[q][t]], axis=1) * done[t]
            done.append(acc * jnp.concatenate([s, s], axis=1))
        u = done[0]
        for q in range(1, 8):
            u = jnp.where(sub == q, done[q], u)
        work[o:o + 8, :] = u
        if o + 8 < HALF:
            h, m, l = split3(u)
            left = jnp.concatenate([v[:, :HALF] for v in (h, h, m, h, l, m)], axis=0).astype(BF16)
            right = jnp.concatenate([h, m, h, l, h, m], axis=0).astype(BF16)
            update = lax.dot_general(
                left, right, (((0,), (0,)), ((), ())), preferred_element_type=F32
            )
            work[o + 8:, :] = work[o + 8:, :] - update[o + 8:, :]


def leaf_factor(work, block):
    ri = lax.broadcasted_iota(jnp.int32, (HALF, HALF), 0)
    ci = lax.broadcasted_iota(jnp.int32, (HALF, HALF), 1)
    work[:, :HALF] = block
    work[:, HALF:] = jnp.where(ri == ci, 1.0, 0.0).astype(F32)
    leaf(work)
    upper = jnp.where(ci >= ri, work[:, :HALF], 0.0)
    inverse = jnp.where(ci <= ri, work[:, HALF:], 0.0)
    return upper, inverse


def block_factor(k, s, work, linv, n):
    here = pl.ds(pl.multiple_of(k * BLK, BLK), BLK)
    block = s[k, here, :]
    u1, inv1 = leaf_factor(work, block[:HALF, :HALF])
    l21 = dot_nt(block[HALF:, :HALF], inv1)
    u2, inv2 = leaf_factor(work, block[HALF:, HALF:] - dot_nt(l21, l21))
    inv21 = -dot_nn(inv2, dot_nn(l21, inv1))
    zero = jnp.zeros((HALF, HALF), F32)
    linv[n, :HALF, :HALF] = inv1
    linv[n, :HALF, HALF:] = zero
    linv[n, HALF:, :HALF] = inv21
    linv[n, HALF:, HALF:] = inv2
    s[k, here, :] = jnp.concatenate(
        [jnp.concatenate([u1.T, zero], axis=1), jnp.concatenate([l21, u2.T], axis=1)], axis=0
    )


def rows_of(i):
    return pl.ds(pl.multiple_of(i * BLK, BLK), BLK)


FB = 4
MASKS = ((4017, 192, 560, 16), (8, 49160, 34944, 50377), (49152, 7937, 12544, 6400))


def first_id(k):
    return 4 * k - lax.div(k * (k - 1), jnp.int32(2))


def kernel(tiles, out, w, v, v10, t, lb, s, work, ph, pw, vh, vw,
           load, load_t, c_recv, d_recv, e_recv, r_own, r_sib, l_own, l_sib,
           c_send, d_send, e_send, r_send, a_send, b_send, s_send, root_send, osem):
    r = lax.axis_index("row")
    c = lax.axis_index("col")
    x = lax.div(r, 4)
    z = lax.rem(r, 4)
    y = lax.div(c, 2)
    core = lax.rem(c, 2)
    sibling = (r, c + 1 - 2 * core)
    dirs = (
        (lax.rem(x + 1, 4) * 4 + z, c),
        (lax.rem(x + 3, 4) * 4 + z, c),
        (x * 4 + lax.rem(z + 1, 4), c),
        (x * 4 + lax.rem(z + 3, 4), c),
    )
    is_f = (r == 0) & (c == 0)
    is_g = (r == 1) & (c == 1)
    plain = jnp.logical_not(is_f | is_g)
    full = (r >= 2) & (r <= 10)
    in_a = r != 1
    in_b = r != 0
    slot_a = jnp.where(c >= 2, 0, 1)
    mirror = x * 4 + lax.rem(5 - z, 4)

    def bit(mask, pos):
        return lax.rem(lax.shift_right_logical(jnp.int32(mask), pos), 2)

    flags_a = [[bit(m[d], r) for d in range(4)] for m in MASKS]
    flags_b = [[bit(m[d], mirror) for d in (0, 1, 3, 2)] for m in MASKS]

    def remote(src, dst, send, recv, device):
        return pltpu.make_async_remote_copy(
            src_ref=src, dst_ref=dst, send_sem=send, recv_sem=recv,
            device_id=device, device_id_type=pl.DeviceIdType.MESH,
        )

    def arrived(ref, sem):
        pltpu.make_async_copy(ref, ref, sem).wait()

    def drain(sem, rows):
        ref = t.at[0, pl.ds(0, rows)]
        pltpu.make_async_copy(ref, ref, sem).wait()

    def forward(flags, n, ref, sends, recv):
        tree = lax.rem(n, 3)
        for d in range(4):
            go = jnp.where(tree == 0, flags[0][d], jnp.where(tree == 1, flags[1][d], flags[2][d]))

            @pl.when(go == 1)
            def _():
                remote(ref, ref, sends.at[tree, d], recv, dirs[d]).start()

    def drain_tree(flags, sends, rows):
        for tree in range(3):
            for d in range(4):
                @pl.when(flags[tree][d] == 1)
                def _():
                    drain(sends.at[tree, d], rows[tree])

    barrier = pltpu.get_barrier_semaphore()
    for n in range(1, 8):
        pl.semaphore_signal(barrier, inc=1, device_id=(r, lax.rem(c + n, 8)),
                            device_id_type=pl.DeviceIdType.MESH)
    for d in range(4):
        pl.semaphore_signal(barrier, inc=1, device_id=dirs[d], device_id_type=pl.DeviceIdType.MESH)

    @pl.when(is_f | is_g)
    def _():
        pl.semaphore_signal(barrier, inc=1, device_id=(1 - r, 1 - c), device_id_type=pl.DeviceIdType.MESH)

    def block_cols(n):
        return pl.ds(pl.multiple_of(n * BLK, BLK), BLK)

    def local(src, dst, sem):
        return pltpu.make_async_copy(src, dst, sem)

    @pl.when(is_f | is_g)
    def _():
        for k in range(FB):
            local(tiles.at[0, pl.ds(k * BLK, TILE - k * BLK), pl.ds(k * BLK, BLK)],
                  s.at[k, pl.ds(k * BLK, TILE - k * BLK), :], load.at[4 + k]).start()
            if k:
                s[k, pl.ds(0, k * BLK), :] = jnp.zeros((k * BLK, BLK), F32)

    def tile_rows(base):
        return [local(tiles.at[slot_a, pl.ds(k * BLK, BLK), :], v.at[base + k], load.at[k]) for k in range(FB)]

    def extra_rows():
        return [local(tiles.at[1, pl.ds(k * BLK, BLK), :], v10.at[k], load.at[8 + k]) for k in range(FB)]

    def own_cols():
        return [local(tiles.at[0, :, pl.ds(k * BLK, BLK)], w.at[4 * core + k], load.at[k]) for k in range(FB)]

    def target(n):
        return local(tiles.at[slot_a if n == 0 else 1], t.at[n], load_t.at[n])

    def pass_on():
        return [local(tiles.at[n], out.at[n], osem.at[n]) for n in range(2)]

    @pl.when(r == 0)
    def _():
        for cp in tile_rows(0):
            cp.start()

    @pl.when(r == 1)
    def _():
        for cp in tile_rows(4):
            cp.start()

        @pl.when(c == 2)
        def _():
            for cp in extra_rows():
                cp.start()

    @pl.when(full & (y == 0))
    def _():
        for cp in own_cols():
            cp.start()

    @pl.when(r >= 11)
    def _():
        for cp in pass_on():
            cp.start()

    @pl.when(plain)
    def _():
        pl.semaphore_wait(barrier, 11)

    @pl.when(is_f | is_g)
    def _():
        pl.semaphore_wait(barrier, 12)

    @pl.when((full & (y == 0)) | ((r == 1) & (c == 0)))
    def _():
        for k in range(FB):
            remote(tiles.at[0, :, pl.ds(k * BLK, BLK)], w.at[4 * core + k],
                   r_send.at[2], r_sib.at[k], sibling).start()

    @pl.when(r == 0)
    def _():
        for cp in tile_rows(0):
            cp.wait()

    @pl.when(r == 1)
    def _():
        for cp in tile_rows(4):
            cp.wait()

        @pl.when(c == 2)
        def _():
            for cp in extra_rows():
                cp.wait()

    @pl.when(full)
    def _():
        target(0).start()

        @pl.when(c == 2)
        def _():
            target(1).start()

    def quarter(n):
        return pl.ds(pl.multiple_of(lax.rem(n, 4) * 64, 64), 64)

    def c_event(n):
        ref = v.at[lax.div(n, 4), quarter(n), :]

        @pl.when(in_a & (r != 0))
        def _():
            arrived(ref, c_recv.at[n])

        forward(flags_a, n, ref, c_send, c_recv.at[n])

    def d_event(n):
        ref = v.at[4 + lax.div(n, 4), quarter(n), :]

        @pl.when(in_b & (r != 1))
        def _():
            arrived(ref, d_recv.at[n])

        forward(flags_b, n, ref, d_send, d_recv.at[n])

    def e_event(n):
        ref = v10.at[lax.div(n, 4), quarter(n), :]

        @pl.when(c == 2)
        def _():
            @pl.when(in_b & (r != 1))
            def _():
                arrived(ref, e_recv.at[n])

            forward(flags_b, n, ref, e_send, e_recv.at[n])

    half_512 = pl.ds(pl.multiple_of(core * 512, 512), 512)
    other_512 = pl.ds(pl.multiple_of(512 - core * 512, 512), 512)

    def r_event(n):
        @pl.when(full)
        def _():
            ref = w.at[n, half_512, :]
            m = lax.rem(n, 4)

            @pl.when(y == 0)
            def _():
                @pl.when(lax.div(n, 4) == core)
                def _():
                    arrived(w.at[n], load.at[m])

                @pl.when(lax.div(n, 4) != core)
                def _():
                    arrived(w.at[n], r_sib.at[m])

                remote(ref, ref, r_send.at[0], r_own.at[n], (r, 2 + core)).start()
                remote(ref, ref, r_send.at[1], r_own.at[n], (r, 6 + core)).start()

            @pl.when(y != 0)
            def _():
                arrived(ref, r_own.at[n])
                remote(ref, ref, r_send.at[2], r_sib.at[n], sibling).start()

                @pl.when((y + 2 * lax.rem(n, 2) == 1) | ((y == 3) & (lax.rem(n, 2) == 1)))
                def _():
                    remote(ref, ref, r_send.at[0], r_own.at[n], (r, 4 + core)).start()

    half_128 = pl.ds(pl.multiple_of(core * HALF, HALF), HALF)
    other_128 = pl.ds(pl.multiple_of(HALF - core * HALF, HALF), HALF)

    def l_event(n, flags, member, sends):
        ref = lb.at[n, half_128, :]

        @pl.when(member)
        def _():
            arrived(ref, l_own.at[n])

            @pl.when(full)
            def _():
                remote(ref, ref, s_send, l_sib.at[n], sibling).start()

            forward(flags, n, ref, sends, l_own.at[n])

    def l_ready(n):
        arrived(lb.at[n, other_128, :], l_sib.at[n])

    def a_events(k):
        lo = first_id(k)

        @pl.loop(lo, lo + 4 - k)
        def _(n):
            l_event(n, flags_a, in_a, a_send)

        @pl.when(full)
        def _():
            @pl.loop(lo, lo + 4 - k)
            def _(n):
                l_ready(n)

    def b_events(lo, count):
        @pl.loop(lo, lo + count)
        def _(n):
            l_event(n, flags_b, in_b, b_send)

        @pl.when(full)
        def _():
            @pl.loop(lo, lo + count)
            def _(n):
                l_ready(n)

    def chain(base, send):
        @pl.loop(0, FB)
        def _(k):
            lo = base + first_id(k)
            block_factor(k, s, work, lb, lo)
            send(lo)

            @pl.loop(k + 1, FB)
            def _(i):
                p = dot_nt(s[k, rows_of(i), :], lb[lo])
                s[k, rows_of(i), :] = p
                lb[lo + i - k] = p
                send(lo + i - k)

            @pl.loop(k + 1, FB)
            def _(j):
                @pl.loop(j, FB)
                def _(i):
                    s[j, rows_of(i), :] = s[j, rows_of(i), :] - dot_nt(s[k, rows_of(i), :], s[k, rows_of(j), :])

    def half_of(core_no):
        return pl.ds(core_no * HALF, HALF)

    def send_f(n):
        for q, h in enumerate((0, 1)):
            remote(lb.at[n, half_of(h), :], lb.at[n, half_of(h), :], root_send.at[8 + q],
                   (l_own if h == 1 else l_sib).at[n], (1, 1)).start()
        for other in range(1, 8):
            ref = lb.at[n, half_of(other % 2), :]
            remote(ref, ref, root_send.at[other], l_own.at[n], (0, other)).start()
        forward(flags_a, n, lb.at[n, half_of(0), :], a_send, l_own.at[n])

    def send_g(n, both):
        for other in (0, 2, 3, 4, 5, 6, 7):
            ref = lb.at[n, half_of(other % 2), :]
            remote(ref, ref, root_send.at[other], l_own.at[n], (1, other)).start()
        if both:
            ref = lb.at[n, half_of(1), :]
            remote(ref, ref, root_send.at[8], l_sib.at[n], (1, 0)).start()
        forward(flags_b, n, lb.at[n, half_of(1), :], b_send, l_own.at[n])

    def factor_out():
        return [local(s.at[k], out.at[0, :, pl.ds(k * BLK, BLK)], osem.at[2 + k]) for k in range(FB)]

    @pl.when(is_f)
    def _():
        for k in range(FB):
            arrived(s.at[k, pl.ds(k * BLK, TILE - k * BLK), :], load.at[4 + k])

        @pl.loop(0, 16)
        def _(n):
            c_event(n)

        chain(0, send_f)
        for cp in factor_out():
            cp.start()
        for cp in factor_out():
            cp.wait()
        drain_tree(flags_a, c_send, (384, 320, 320))
        for other in range(1, 10):
            drain(root_send.at[other], 320)

    @pl.when(is_g)
    def _():
        for k in range(FB):
            arrived(s.at[k, pl.ds(k * BLK, TILE - k * BLK), :], load.at[4 + k])
            arrived(w.at[k], r_sib.at[k])

        @pl.loop(0, 16)
        def _(n):
            d_event(n)

        @pl.loop(0, FB)
        def _(k):
            lo = first_id(k)

            @pl.loop(lo, lo + 4 - k)
            def _(n):
                arrived(lb.at[n, half_of(1), :], l_own.at[n])
                arrived(lb.at[n, half_of(0), :], l_sib.at[n])

            @pl.loop(0, FB)
            def _(i):
                p = dot_nt(w[k, rows_of(i), :], lb[lo])
                w[k, rows_of(i), :] = p
                lb[10 + 4 * k + i] = p
                send_g(10 + 4 * k + i, True)

            @pl.loop(0, FB)
            def _(j):
                @pl.loop(j, FB)
                def _(i):
                    s[j, rows_of(i), :] = s[j, rows_of(i), :] - dot_nt(w[k, rows_of(i), :], w[k, rows_of(j), :])

            @pl.loop(k + 1, FB)
            def _(j):
                @pl.loop(0, FB)
                def _(i):
                    w[j, rows_of(i), :] = w[j, rows_of(i), :] - dot_nt(w[k, rows_of(i), :], lb[lo + j - k])

        chain(26, lambda n: send_g(n, False))
        for cp in factor_out():
            cp.start()
        for cp in factor_out():
            cp.wait()
        drain_tree(flags_b, d_send, (384, 320, 320))
        for other in (0, 2, 3, 4, 5, 6, 7):
            drain(root_send.at[other], 832)
        drain(root_send.at[8], 512)

    def v_split(buf, k):
        hi, lo = split2(buf[k])
        vh[...] = hi
        vw[...] = lo

    def v_solve(buf, k, n):
        buf[k] = dot3(split2(lb[n]), split2(buf[k]), 0)
        v_split(buf, k)

    def v_sub(buf, j, n):
        buf[j] = buf[j] - dot3(split2(lb[n]), (vh[...], vw[...]), 0)

    def w_solve(k, n):
        w[k] = dot3(split2(w[k]), split2(lb[n]), 1)
        hi, lo = split2(w[k])
        ph[...] = hi
        pw[...] = lo

    def w_sub(j, n):
        w[j] = w[j] - dot3((ph[...], pw[...]), split2(lb[n]), 1)

    def t_sub(slot):
        for n in range(4):
            cols = pl.ds(n * BLK, BLK)
            t[slot, :, cols] = t[slot, :, cols] - dot3((ph[...], pw[...]), (vh[:, cols], vw[:, cols]), 0)

    @pl.when(plain)
    def _():
        @pl.loop(0, FB)
        def _(g):
            @pl.loop(4 * g, 4 * g + 4)
            def _(n):
                c_event(n)

            r_event(g)

        drain_tree(flags_a, c_send, (384, 320, 320))

        @pl.loop(0, FB)
        def _(k):
            a_events(k)

            @pl.loop(4 * k, 4 * k + 4)
            def _(n):
                d_event(n)
                e_event(n)

            @pl.when(full)
            def _():
                lo = first_id(k)
                v_solve(v, k, lo)

                @pl.loop(k + 1, FB)
                def _(j):
                    v_sub(v, j, lo + j - k)

            b_events(10 + 4 * k, 4)
            r_event(4 + k)

        drain_tree(flags_b, d_send, (384, 320, 320))

        @pl.when(c == 2)
        def _():
            drain_tree(flags_b, e_send, (384, 320, 320))

    @pl.when(full)
    def _():
        @pl.when(y == 0)
        def _():
            drain(r_send.at[0], 1024)
            drain(r_send.at[1], 1024)

        @pl.when((y == 1) | (y == 3))
        def _():
            drain(r_send.at[0], 512)

        drain(r_send.at[2], 1024)

        @pl.when(y != 0)
        def _():
            @pl.loop(0, NB)
            def _(n):
                arrived(w.at[n, other_512, :], r_sib.at[n])

        target(0).wait()

        @pl.when(c == 2)
        def _():
            target(1).wait()

    @pl.when((r == 1) & (c == 0))
    def _():
        drain(r_send.at[2], 1024)

    @pl.when(plain)
    def _():
        @pl.loop(0, FB)
        def _(k):
            lo = first_id(k)

            @pl.when(full)
            def _():
                v_split(v, k)

                @pl.loop(0, FB)
                def _(j):
                    v_sub(v, 4 + j, 10 + 4 * k + j)

                w_solve(k, lo)

                @pl.loop(k + 1, FB)
                def _(j):
                    w_sub(j, lo + j - k)

                @pl.loop(0, FB)
                def _(j):
                    w_sub(4 + j, 10 + 4 * k + j)

                t_sub(0)

            @pl.when(lax.rem(k, 2) == 1)
            def _():
                q = lax.div(k, 2)
                b_events(26 + first_id(q), 4 - q)

        @pl.loop(0, FB)
        def _(k):
            lo = 26 + first_id(k)

            @pl.when(k >= 2)
            def _():
                b_events(lo, 4 - k)

            @pl.when(full)
            def _():
                w_solve(4 + k, lo)

                @pl.loop(k + 1, FB)
                def _(j):
                    w_sub(4 + j, lo + j - k)

                @pl.when(c == 2)
                def _():
                    v_solve(v10, k, lo)

                    @pl.loop(k + 1, FB)
                    def _(j):
                        v_sub(v10, j, lo + j - k)

                    t_sub(1)

                v_solve(v, 4 + k, lo)

                @pl.loop(k + 1, FB)
                def _(j):
                    v_sub(v, 4 + j, lo + j - k)

                t_sub(0)

    def run(copies):
        for cp in copies:
            cp.start()
        for cp in copies:
            cp.wait()

    @pl.when(full)
    def _():
        main = local(t.at[0], out.at[slot_a], osem.at[0])

        @pl.when(c < 2)
        def _():
            run([main] + [local(w.at[4 * c + k], out.at[0, :, pl.ds(k * BLK, BLK)], osem.at[2 + k])
                          for k in range(FB)])

        @pl.when(c == 2)
        def _():
            run([main, local(t.at[1], out.at[1], osem.at[1])])

        @pl.when(c > 2)
        def _():
            run([main, local(tiles.at[1], out.at[1], osem.at[1])])

        sent = t.at[:, pl.ds(0, 576)]
        arrived(sent, s_send)

    @pl.when(r >= 11)
    def _():
        for cp in pass_on():
            cp.wait()

    @pl.when(r < 2)
    def _():
        t[0] = jnp.zeros((TILE, TILE), F32)
        blank = [local(t.at[0], out.at[n], osem.at[n]) for n in range(2)]

        @pl.when(c <= r)
        def _():
            run(blank[1:])

        @pl.when(c > r)
        def _():
            run(blank)

    @pl.when((r == 1) & (c == 0))
    def _():
        @pl.loop(10, 26)
        def _(n):
            arrived(lb.at[n, half_of(1), :], l_sib.at[n])

        panel = [local(lb.at[10 + 4 * k + j], out.at[0, pl.ds(j * BLK, BLK), pl.ds(k * BLK, BLK)],
                       osem.at[6 + 4 * k + j]) for k in range(FB) for j in range(FB)]
        run(panel)

    drain_tree(flags_a, a_send, (128, 96, 96))
    drain_tree(flags_b, b_send, (256, 288, 288))


def on_device(kernel_tiles, profile):
    tiles = kernel_tiles.reshape(2, TILE, TILE)
    dma = pltpu.SemaphoreType.DMA
    out = pl.pallas_call(
        kernel,
        out_shape=jax.ShapeDtypeStruct((2, TILE, TILE), F32),
        in_specs=[pl.BlockSpec(memory_space=pl.ANY)],
        out_specs=pl.BlockSpec(memory_space=pl.ANY),
        scratch_shapes=[
            pltpu.VMEM((NB, TILE, BLK), F32),
            pltpu.VMEM((NB, BLK, TILE), F32),
            pltpu.VMEM((FB, BLK, TILE), F32),
            pltpu.VMEM((2, TILE, TILE), F32),
            pltpu.VMEM((36, BLK, BLK), F32),
            pltpu.VMEM((FB, TILE, BLK), F32),
            pltpu.VMEM((HALF, 2 * HALF), F32),
            pltpu.VMEM((TILE, BLK), BF16),
            pltpu.VMEM((TILE, BLK), BF16),
            pltpu.VMEM((BLK, TILE), BF16),
            pltpu.VMEM((BLK, TILE), BF16),
            dma((12,)), dma((2,)),
            dma((16,)), dma((16,)), dma((16,)),
            dma((8,)), dma((8,)), dma((36,)), dma((36,)),
            dma((3, 4)), dma((3, 4)), dma((3, 4)), dma((3,)),
            dma((3, 4)), dma((3, 4)), dma, dma((10,)), dma((22,)),
        ],
        compiler_params=pltpu.CompilerParams(
            vmem_limit_bytes=58 * 2**20, collective_id=0, has_side_effects=True
        ),
        name="panel_steps",
    )(tiles)
    return out.reshape(kernel_tiles.shape)


def solution(mesh):
    placed = (P(None, "row", None, "col", None, None), P())
    return jax.shard_map(
        on_device,
        mesh=mesh,
        in_specs=placed,
        out_specs=P(None, "row", None, "col", None, None),
        check_vma=False,
    )
```

time: 745 us -> 974 us (1.31)
  the two profiles are of different devices: /device:TPU:6 before, /device:TPU:11 now
where the time goes in v2:
time: 974 us; the launch traced here: 973 us
  Pallas kernels  965 us (99%)
    pallas_call x1, Pallas kernels, on_device(): pl.pallas_call(kernel, out_shape=jax.ShapeDtypeStruct((2, TILE, TILE), F3...  965 us

profile of v2, /device:TPU:11, one launch (start us, length us, event | category | flops | bytes accessed | tf_op | source)
XLA Modules:
  0.0 973.4 jit_solution(1204474886279746153)
XLA Ops:
  0.0 965.0 %panel_steps.1 = f32[2,1024,1024]{2,1,0:T(8,128)} custom-call(f32[2,1024,1024]{2,1,0:T(8,128)} %bitcast.5), custom_call_target="tpu_custom_call" | custom-call | tf_op jit(solution)/shard_map/panel_steps/pallas_call | solution.py:724
  965.0 8.4 copy.4

commit v3 on v2

--- a/solution.py
+++ b/solution.py
@@ -116,7 +116,8 @@
 
 
 FB = 4
-MASKS = ((4017, 192, 560, 16), (8, 49160, 34944, 50377), (49152, 7937, 12544, 6400))
+SLOTS = 38
+EXTRA_SLOTS = 46
 
 
 def first_id(k):
@@ -125,7 +126,7 @@
 
 def kernel(tiles, out, w, v, v10, t, lb, s, work, ph, pw, vh, vw,
            load, load_t, c_recv, d_recv, e_recv, r_own, r_sib, l_own, l_sib,
-           c_send, d_send, e_send, r_send, a_send, b_send, s_send, root_send, osem):
+           c_send, d_send, e_send, r_send, a_send, b_send, y_send, s_send, root_send, osem):
     r = lax.axis_index("row")
     c = lax.axis_index("col")
     x = lax.div(r, 4)
@@ -143,16 +144,30 @@
     is_g = (r == 1) & (c == 1)
     plain = jnp.logical_not(is_f | is_g)
     full = (r >= 2) & (r <= 10)
-    in_a = r != 1
-    in_b = r != 0
     slot_a = jnp.where(c >= 2, 0, 1)
-    mirror = x * 4 + lax.rem(5 - z, 4)
-
-    def bit(mask, pos):
-        return lax.rem(lax.shift_right_logical(jnp.int32(mask), pos), 2)
-
-    flags_a = [[bit(m[d], r) for d in range(4)] for m in MASKS]
-    flags_b = [[bit(m[d], mirror) for d in (0, 1, 3, 2)] for m in MASKS]
+    never = r < 0
+
+    c_out = (((x <= 1) & (z == 0)), never, ((x == 1) | (x == 2)) & (z <= 1),
+             ((x == 0) & ((z == 0) | (z == 3))) | ((x == 1) & (z == 0)))
+    c_in = jnp.logical_not((x == 3) | ((x == 0) & (z == 1)) | ((x == 2) & (z == 3)))
+    c_depth = jnp.where(x == 0, lax.rem(4 - z, 4), jnp.where(x == 1, 1 + jnp.minimum(z, 4 - z), 2 + z))
+    d_out = (((x == 0) & (z >= 1)) | ((x == 1) & ((z == 1) | (z == 2))), never,
+             (x == 0) & ((z == 1) | (z == 2)), ((x == 1) | (x == 2)) & (z == 1))
+    d_in = jnp.logical_not((x == 3) | ((x == 0) & (z == 0)) | ((x == 2) & (z == 3)))
+    d_depth = jnp.where(x == 0, z - 1, jnp.where(x == 1, jnp.where(z == 0, 2, z), jnp.where(z == 1, 2, 3)))
+
+    def stream_tree(z0):
+        dz = lax.rem(z + 4 - z0, 4)
+        root = (x == 0) & (z == z0)
+        turn = jnp.minimum(dz, 4 - dz)
+        outs = (root | (x == 2) | (x == 3), (x == 3) & (z >= 2), (x == 3) & (dz <= 1), (x == 3) & (dz == 0))
+        outs = (outs[1], outs[0], outs[2], outs[3])
+        depth = jnp.where(root, 0, jnp.where(x == 0, 2, 4 - x) + turn)
+        return outs, (x >= 1) | (z >= 2) | root, depth
+
+    y_depth = jnp.where(y == 0, 0, jnp.where(y == 2, 2, 1))
+    a_out, a_in, a_depth = stream_tree(0)
+    b_out, b_in, b_depth = stream_tree(1)
 
     def remote(src, dst, send, recv, device):
         return pltpu.make_async_remote_copy(
@@ -167,21 +182,17 @@
         ref = t.at[0, pl.ds(0, rows)]
         pltpu.make_async_copy(ref, ref, sem).wait()
 
-    def forward(flags, n, ref, sends, recv):
-        tree = lax.rem(n, 3)
+    def forward(outs, ref, sends, recv):
         for d in range(4):
-            go = jnp.where(tree == 0, flags[0][d], jnp.where(tree == 1, flags[1][d], flags[2][d]))
-
-            @pl.when(go == 1)
-            def _():
-                remote(ref, ref, sends.at[tree, d], recv, dirs[d]).start()
-
-    def drain_tree(flags, sends, rows):
-        for tree in range(3):
-            for d in range(4):
-                @pl.when(flags[tree][d] == 1)
-                def _():
-                    drain(sends.at[tree, d], rows[tree])
+            @pl.when(outs[d])
+            def _():
+                remote(ref, ref, sends(d), recv, dirs[d]).start()
+
+    def drain_outs(outs, sends, rows):
+        for d in range(4):
+            @pl.when(outs[d])
+            def _():
+                drain(sends(d), rows)
 
     barrier = pltpu.get_barrier_semaphore()
     for n in range(1, 8):
@@ -220,8 +231,11 @@
     def target(n):
         return local(tiles.at[slot_a if n == 0 else 1], t.at[n], load_t.at[n])
 
-    def pass_on():
-        return [local(tiles.at[n], out.at[n], osem.at[n]) for n in range(2)]
+    def pass_in(n):
+        return local(tiles.at[n], t.at[n], load_t.at[n])
+
+    def pass_out(n):
+        return local(t.at[n], out.at[n], osem.at[n])
 
     @pl.when(r == 0)
     def _():
@@ -245,8 +259,12 @@
 
     @pl.when(r >= 11)
     def _():
-        for cp in pass_on():
-            cp.start()
+        pass_in(0).start()
+        pass_in(1).start()
+
+    @pl.when(full & (c > 2))
+    def _():
+        pass_in(1).start()
 
     @pl.when(plain)
     def _():
@@ -260,7 +278,7 @@
     def _():
         for k in range(FB):
             remote(tiles.at[0, :, pl.ds(k * BLK, BLK)], w.at[4 * core + k],
-                   r_send.at[2], r_sib.at[k], sibling).start()
+                   r_send.at[2, 4 * core + k], r_sib.at[k], sibling).start()
 
     @pl.when(r == 0)
     def _():
@@ -277,6 +295,17 @@
             for cp in extra_rows():
                 cp.wait()
 
+    @pl.when(r >= 11)
+    def _():
+        for n in range(2):
+            pass_in(n).wait()
+            pass_out(n).start()
+
+    @pl.when(full & (c > 2))
+    def _():
+        pass_in(1).wait()
+        pass_out(1).start()
+
     @pl.when(full)
     def _():
         target(0).start()
@@ -285,111 +314,147 @@
         def _():
             target(1).start()
 
-    def quarter(n):
-        return pl.ds(pl.multiple_of(lax.rem(n, 4) * 64, 64), 64)
+    def within(n, count):
+        return (n >= 0) & (n < count)
 
     def c_event(n):
-        ref = v.at[lax.div(n, 4), quarter(n), :]
-
-        @pl.when(in_a & (r != 0))
+        k = lax.div(n, 8)
+        ref = v.at[k, pl.ds(pl.multiple_of(lax.rem(n, 8) * 32, 32), 32), :]
+
+        @pl.when(r != 0)
         def _():
             arrived(ref, c_recv.at[n])
 
-        forward(flags_a, n, ref, c_send, c_recv.at[n])
+        forward(c_out, ref, lambda d: c_send.at[d, k], c_recv.at[n])
 
     def d_event(n):
-        ref = v.at[4 + lax.div(n, 4), quarter(n), :]
-
-        @pl.when(in_b & (r != 1))
+        k = lax.div(n, 8)
+        ref = v.at[4 + k, pl.ds(pl.multiple_of(lax.rem(n, 8) * 32, 32), 32), :]
+
+        @pl.when(r != 1)
         def _():
             arrived(ref, d_recv.at[n])
 
-        forward(flags_b, n, ref, d_send, d_recv.at[n])
-
-    def e_event(n):
-        ref = v10.at[lax.div(n, 4), quarter(n), :]
-
-        @pl.when(c == 2)
-        def _():
-            @pl.when(in_b & (r != 1))
-            def _():
-                arrived(ref, e_recv.at[n])
-
-            forward(flags_b, n, ref, e_send, e_recv.at[n])
-
-    half_512 = pl.ds(pl.multiple_of(core * 512, 512), 512)
-    other_512 = pl.ds(pl.multiple_of(512 - core * 512, 512), 512)
+        forward(d_out, ref, lambda d: d_send.at[d], d_recv.at[n])
+
+    def e_ref(n):
+        return v10.at[lax.div(n, 4), pl.ds(pl.multiple_of(lax.rem(n, 4) * 64, 64), 64), :]
+
+    def e_even(m):
+        n = 2 * m
+
+        @pl.when(r != 1)
+        def _():
+            arrived(e_ref(n), e_recv.at[n])
+
+        forward(d_out, e_ref(n), lambda d: e_send.at[0, d], e_recv.at[n])
+
+    def e_odd(m):
+        n = 2 * m + 1
+
+        @pl.when(r != 1)
+        def _():
+            arrived(e_ref(n), e_recv.at[n])
+
+        forward(c_out[:3] + (c_out[3] | (r == 1),), e_ref(n), lambda d: e_send.at[1, d], e_recv.at[n])
+
+    def r_rows(n, half):
+        return pl.ds(pl.multiple_of(half * 512 + lax.rem(n, 4) * 128, 128), 128)
 
     def r_event(n):
-        @pl.when(full)
-        def _():
-            ref = w.at[n, half_512, :]
-            m = lax.rem(n, 4)
-
-            @pl.when(y == 0)
-            def _():
-                @pl.when(lax.div(n, 4) == core)
+        b = lax.div(n, 4)
+        ref = w.at[b, r_rows(n, core), :]
+
+        @pl.when(y == 0)
+        def _():
+            m = lax.rem(b, 4)
+
+            @pl.when(lax.rem(n, 4) == 0)
+            def _():
+                @pl.when(lax.div(b, 4) == core)
                 def _():
-                    arrived(w.at[n], load.at[m])
-
-                @pl.when(lax.div(n, 4) != core)
+                    arrived(w.at[b], load.at[m])
+
+                @pl.when(lax.div(b, 4) != core)
                 def _():
-                    arrived(w.at[n], r_sib.at[m])
-
-                remote(ref, ref, r_send.at[0], r_own.at[n], (r, 2 + core)).start()
-                remote(ref, ref, r_send.at[1], r_own.at[n], (r, 6 + core)).start()
-
-            @pl.when(y != 0)
-            def _():
-                arrived(ref, r_own.at[n])
-                remote(ref, ref, r_send.at[2], r_sib.at[n], sibling).start()
-
-                @pl.when((y + 2 * lax.rem(n, 2) == 1) | ((y == 3) & (lax.rem(n, 2) == 1)))
-                def _():
-                    remote(ref, ref, r_send.at[0], r_own.at[n], (r, 4 + core)).start()
+                    arrived(w.at[b], r_sib.at[m])
+
+            remote(ref, ref, r_send.at[0, b], r_own.at[n], (r, 2 + core)).start()
+            remote(ref, ref, r_send.at[1, b], r_own.at[n], (r, 6 + core)).start()
+
+        @pl.when(y != 0)
+        def _():
+            arrived(ref, r_own.at[n])
+            remote(ref, ref, r_send.at[2, b], r_sib.at[n], sibling).start()
+            odd = lax.rem(n, 2)
+
+            @pl.when(((y == 1) & (odd == 0)) | ((y == 3) & (odd == 1)))
+            def _():
+                remote(ref, ref, r_send.at[0, b], r_own.at[n], (r, 4 + core)).start()
+
+    def w_ready(b):
+        @pl.when(y == 0)
+        def _():
+            drain(r_send.at[0, b], 128)
+            drain(r_send.at[1, b], 128)
+
+            @pl.when(lax.div(b, 4) == core)
+            def _():
+                drain(r_send.at[2, b], 256)
+
+        @pl.when(y != 0)
+        def _():
+            drain(r_send.at[2, b], 128)
+
+            @pl.when(y != 2)
+            def _():
+                drain(r_send.at[0, b], 64)
+
+            @pl.loop(4 * b, 4 * b + 4)
+            def _(n):
+                arrived(w.at[b, r_rows(n, 1 - core), :], r_sib.at[n])
 
     half_128 = pl.ds(pl.multiple_of(core * HALF, HALF), HALF)
     other_128 = pl.ds(pl.multiple_of(HALF - core * HALF, HALF), HALF)
 
-    def l_event(n, flags, member, sends):
+    def l_event(n, outs, sends, root_row):
         ref = lb.at[n, half_128, :]
-
-        @pl.when(member)
-        def _():
-            arrived(ref, l_own.at[n])
-
-            @pl.when(full)
-            def _():
-                remote(ref, ref, s_send, l_sib.at[n], sibling).start()
-
-            forward(flags, n, ref, sends, l_own.at[n])
-
-    def l_ready(n):
-        arrived(lb.at[n, other_128, :], l_sib.at[n])
-
-    def a_events(k):
-        lo = first_id(k)
-
-        @pl.loop(lo, lo + 4 - k)
+        arrived(ref, l_own.at[n])
+
+        @pl.when(full)
+        def _():
+            remote(ref, ref, s_send, l_sib.at[n], sibling).start()
+
+        forward(outs, ref, lambda d: sends.at[d], l_own.at[n])
+        odd = lax.rem(n, 2)
+
+        @pl.when((r == root_row) & (((y == 1) & (odd == 0)) | ((y == 3) & (odd == 1))))
+        def _():
+            remote(ref, ref, y_send.at[root_row], l_own.at[n], (r, 4 + core)).start()
+
+    def l_ready(lo, count):
+        @pl.loop(lo, lo + count)
         def _(n):
-            l_event(n, flags_a, in_a, a_send)
-
-        @pl.when(full)
+            arrived(lb.at[n, other_128, :], l_sib.at[n])
+
+    def a_event(n):
+        l_event(n, a_out, a_send, 0)
+
+    def b_event(n):
+        l_event(n, b_out, b_send, 1)
+
+    def last_events(k):
+        lo = 26 + first_id(k)
+
+        @pl.when(b_in)
         def _():
             @pl.loop(lo, lo + 4 - k)
             def _(n):
-                l_ready(n)
-
-    def b_events(lo, count):
-        @pl.loop(lo, lo + count)
-        def _(n):
-            l_event(n, flags_b, in_b, b_send)
+                b_event(n)
 
         @pl.when(full)
         def _():
-            @pl.loop(lo, lo + count)
-            def _(n):
-                l_ready(n)
+            l_ready(lo, 4 - k)
 
     def chain(base, send):
         @pl.loop(0, FB)
@@ -418,19 +483,19 @@
         for q, h in enumerate((0, 1)):
             remote(lb.at[n, half_of(h), :], lb.at[n, half_of(h), :], root_send.at[8 + q],
                    (l_own if h == 1 else l_sib).at[n], (1, 1)).start()
-        for other in range(1, 8):
+        for other in (1, 2, 3, 6, 7):
             ref = lb.at[n, half_of(other % 2), :]
             remote(ref, ref, root_send.at[other], l_own.at[n], (0, other)).start()
-        forward(flags_a, n, lb.at[n, half_of(0), :], a_send, l_own.at[n])
+        forward(a_out, lb.at[n, half_of(0), :], lambda d: a_send.at[d], l_own.at[n])
 
     def send_g(n, both):
-        for other in (0, 2, 3, 4, 5, 6, 7):
+        for other in (0, 2, 3, 6, 7):
             ref = lb.at[n, half_of(other % 2), :]
             remote(ref, ref, root_send.at[other], l_own.at[n], (1, other)).start()
         if both:
             ref = lb.at[n, half_of(1), :]
             remote(ref, ref, root_send.at[8], l_sib.at[n], (1, 0)).start()
-        forward(flags_b, n, lb.at[n, half_of(1), :], b_send, l_own.at[n])
+        forward(b_out, lb.at[n, half_of(1), :], lambda d: b_send.at[d], l_own.at[n])
 
     def factor_out():
         return [local(s.at[k], out.at[0, :, pl.ds(k * BLK, BLK)], osem.at[2 + k]) for k in range(FB)]
@@ -440,7 +505,7 @@
         for k in range(FB):
             arrived(s.at[k, pl.ds(k * BLK, TILE - k * BLK), :], load.at[4 + k])
 
-        @pl.loop(0, 16)
+        @pl.loop(0, 32)
         def _(n):
             c_event(n)
 
@@ -449,8 +514,10 @@
             cp.start()
         for cp in factor_out():
             cp.wait()
-        drain_tree(flags_a, c_send, (384, 320, 320))
-        for other in range(1, 10):
+        for k in range(FB):
+            drain_outs(c_out, lambda d: c_send.at[d, k], 256)
+        drain_outs(a_out, lambda d: a_send.at[d], 320)
+        for other in (1, 2, 3, 6, 7, 8, 9):
             drain(root_send.at[other], 320)
 
     @pl.when(is_g)
@@ -459,7 +526,7 @@
             arrived(s.at[k, pl.ds(k * BLK, TILE - k * BLK), :], load.at[4 + k])
             arrived(w.at[k], r_sib.at[k])
 
-        @pl.loop(0, 16)
+        @pl.loop(0, 32)
         def _(n):
             d_event(n)
 
@@ -496,169 +563,190 @@
             cp.start()
         for cp in factor_out():
             cp.wait()
-        drain_tree(flags_b, d_send, (384, 320, 320))
-        for other in (0, 2, 3, 4, 5, 6, 7):
+        drain_outs(d_out, lambda d: d_send.at[d], 1024)
+        drain_outs(b_out, lambda d: b_send.at[d], 832)
+        for other in (0, 2, 3, 6, 7):
             drain(root_send.at[other], 832)
         drain(root_send.at[8], 512)
 
-    def v_split(buf, k):
-        hi, lo = split2(buf[k])
+    def low_id(k, m):
+        return jnp.where(
+            k < 4, first_id(m) + k - m,
+            jnp.where(m < 4, 10 + 4 * m + k - 4, 26 + first_id(m - 4) + k - m),
+        )
+
+    def v_sub(buf, at, k, m):
+        buf[k - at] = buf[k - at] - dot3(split2(lb[low_id(k, m)]), split2(buf[m - at]), 0)
+
+    def v_solve(buf, at, k):
+        buf[k - at] = dot3(split2(lb[low_id(k, k)]), split2(buf[k - at]), 0)
+        hi, lo = split2(buf[k - at])
         vh[...] = hi
         vw[...] = lo
 
-    def v_solve(buf, k, n):
-        buf[k] = dot3(split2(lb[n]), split2(buf[k]), 0)
-        v_split(buf, k)
-
-    def v_sub(buf, j, n):
-        buf[j] = buf[j] - dot3(split2(lb[n]), (vh[...], vw[...]), 0)
-
-    def w_solve(k, n):
-        w[k] = dot3(split2(w[k]), split2(lb[n]), 1)
+    def w_sub(k, m):
+        w[k] = w[k] - dot3(split2(w[m]), split2(lb[low_id(k, m)]), 1)
+
+    def w_solve(k):
+        w[k] = dot3(split2(w[k]), split2(lb[low_id(k, k)]), 1)
         hi, lo = split2(w[k])
         ph[...] = hi
         pw[...] = lo
-
-    def w_sub(j, n):
-        w[j] = w[j] - dot3((ph[...], pw[...]), split2(lb[n]), 1)
 
     def t_sub(slot):
         for n in range(4):
             cols = pl.ds(n * BLK, BLK)
             t[slot, :, cols] = t[slot, :, cols] - dot3((ph[...], pw[...]), (vh[:, cols], vw[:, cols]), 0)
 
+    def one_row(k, start):
+        @pl.loop(start, k)
+        def _(m):
+            v_sub(v, 0, k, m)
+            w_sub(k, m)
+
+        v_solve(v, 0, k)
+        w_solve(k)
+        t_sub(0)
+
+    def row_of_first(k):
+        w_ready(k)
+        drain_outs(c_out, lambda d: c_send.at[d, k], 256)
+
+        @pl.loop(0, k + 1)
+        def _(m):
+            l_ready(low_id(k, m), 1)
+
+        @pl.when(k == 0)
+        def _():
+            target(0).wait()
+
+        one_row(k, 0)
+
     @pl.when(plain)
     def _():
-        @pl.loop(0, FB)
-        def _(g):
-            @pl.loop(4 * g, 4 * g + 4)
-            def _(n):
-                c_event(n)
-
-            r_event(g)
-
-        drain_tree(flags_a, c_send, (384, 320, 320))
+        @pl.loop(0, jnp.where(c == 2, EXTRA_SLOTS, SLOTS))
+        def _(slot):
+            n_c = slot - c_depth
+
+            @pl.when(c_in & within(n_c, 32))
+            def _():
+                c_event(n_c)
+
+            n_d = slot - d_depth
+
+            @pl.when(d_in & within(n_d, 32))
+            def _():
+                d_event(n_d)
+
+            n_r = slot - y_depth
+
+            @pl.when(full & within(n_r, 32))
+            def _():
+                r_event(n_r)
+
+            n_a = slot - 7 - a_depth - y_depth
+
+            @pl.when(a_in & within(n_a, 20) & (lax.rem(n_a + 16, 2) == 0))
+            def _():
+                a_event(lax.div(n_a, 2))
+
+            n_b = slot - 13 - b_depth - y_depth
+
+            @pl.when(b_in & within(n_b, 16))
+            def _():
+                b_event(10 + n_b)
+
+            @pl.when(c == 2)
+            def _():
+                n_e = slot - 32 - d_depth
+
+                @pl.when(d_in & within(n_e, 8))
+                def _():
+                    e_even(n_e)
+
+                n_f = slot - 32 - jnp.where(r == 1, 0, 1 + c_depth)
+
+                @pl.when((c_in | (r == 1)) & within(n_f, 8))
+                def _():
+                    e_odd(n_f)
+
+            k = jnp.where(slot == 15, 0, jnp.where(slot == 23, 1, jnp.where(slot == 29, 2, jnp.where(slot == 36, 3, -1))))
+
+            @pl.when(full & (k >= 0))
+            def _():
+                row_of_first(k)
+
+    @pl.when(plain & (r < 2))
+    def _():
+        @pl.when(r == 0)
+        def _():
+            for k in range(FB):
+                drain_outs(c_out, lambda d: c_send.at[d, k], 256)
+
+        @pl.when(r == 1)
+        def _():
+            drain_outs(d_out, lambda d: d_send.at[d], 1024)
+
+    @pl.when(r >= 11)
+    def _():
+        for k in range(FB):
+            drain_outs(c_out, lambda d: c_send.at[d, k], 256)
+        drain_outs(d_out, lambda d: d_send.at[d], 1024)
+
+    @pl.when(c == 2)
+    def _():
+        drain_outs(d_out, lambda d: e_send.at[0, d], 512)
+        drain_outs(c_out[:3] + (c_out[3] | (r == 1),), lambda d: e_send.at[1, d], 512)
+
+    @pl.when(full)
+    def _():
+        drain_outs(d_out, lambda d: d_send.at[d], 1024)
+        l_ready(10, 16)
+
+        @pl.loop(FB, NB)
+        def _(b):
+            w_ready(b)
+
+        @pl.when(c == 2)
+        def _():
+            target(1).wait()
+
+    @pl.when((r == 1) & (c == 0))
+    def _():
+        for k in range(FB):
+            drain(r_send.at[2, k], 256)
+
+    @pl.when(plain)
+    def _():
+        last_events(0)
+
+        @pl.when(full)
+        def _():
+            @pl.loop(FB, NB)
+            def _(k):
+                @pl.loop(0, FB)
+                def _(m):
+                    v_sub(v, 0, k, m)
+                    w_sub(k, m)
 
         @pl.loop(0, FB)
         def _(k):
-            a_events(k)
-
-            @pl.loop(4 * k, 4 * k + 4)
-            def _(n):
-                d_event(n)
-                e_event(n)
+            @pl.when(k > 0)
+            def _():
+                last_events(k)
 
             @pl.when(full)
             def _():
-                lo = first_id(k)
-                v_solve(v, k, lo)
-
-                @pl.loop(k + 1, FB)
-                def _(j):
-                    v_sub(v, j, lo + j - k)
-
-            b_events(10 + 4 * k, 4)
-            r_event(4 + k)
-
-        drain_tree(flags_b, d_send, (384, 320, 320))
-
-        @pl.when(c == 2)
-        def _():
-            drain_tree(flags_b, e_send, (384, 320, 320))
-
-    @pl.when(full)
-    def _():
-        @pl.when(y == 0)
-        def _():
-            drain(r_send.at[0], 1024)
-            drain(r_send.at[1], 1024)
-
-        @pl.when((y == 1) | (y == 3))
-        def _():
-            drain(r_send.at[0], 512)
-
-        drain(r_send.at[2], 1024)
-
-        @pl.when(y != 0)
-        def _():
-            @pl.loop(0, NB)
-            def _(n):
-                arrived(w.at[n, other_512, :], r_sib.at[n])
-
-        target(0).wait()
-
-        @pl.when(c == 2)
-        def _():
-            target(1).wait()
-
-    @pl.when((r == 1) & (c == 0))
-    def _():
-        drain(r_send.at[2], 1024)
-
-    @pl.when(plain)
-    def _():
-        @pl.loop(0, FB)
-        def _(k):
-            lo = first_id(k)
-
-            @pl.when(full)
-            def _():
-                v_split(v, k)
-
-                @pl.loop(0, FB)
-                def _(j):
-                    v_sub(v, 4 + j, 10 + 4 * k + j)
-
-                w_solve(k, lo)
-
-                @pl.loop(k + 1, FB)
-                def _(j):
-                    w_sub(j, lo + j - k)
-
-                @pl.loop(0, FB)
-                def _(j):
-                    w_sub(4 + j, 10 + 4 * k + j)
-
-                t_sub(0)
-
-            @pl.when(lax.rem(k, 2) == 1)
-            def _():
-                q = lax.div(k, 2)
-                b_events(26 + first_id(q), 4 - q)
-
-        @pl.loop(0, FB)
-        def _(k):
-            lo = 26 + first_id(k)
-
-            @pl.when(k >= 2)
-            def _():
-                b_events(lo, 4 - k)
-
-            @pl.when(full)
-            def _():
-                w_solve(4 + k, lo)
-
-                @pl.loop(k + 1, FB)
-                def _(j):
-                    w_sub(4 + j, lo + j - k)
+                one_row(4 + k, 4)
 
                 @pl.when(c == 2)
                 def _():
-                    v_solve(v10, k, lo)
-
-                    @pl.loop(k + 1, FB)
-                    def _(j):
-                        v_sub(v10, j, lo + j - k)
-
+                    @pl.loop(4, 4 + k)
+                    def _(m):
+                        v_sub(v10, 4, 4 + k, m)
+
+                    v_solve(v10, 4, 4 + k)
                     t_sub(1)
-
-                v_solve(v, 4 + k, lo)
-
-                @pl.loop(k + 1, FB)
-                def _(j):
-                    v_sub(v, 4 + j, lo + j - k)
-
-                t_sub(0)
 
     def run(copies):
         for cp in copies:
@@ -681,15 +769,16 @@
 
         @pl.when(c > 2)
         def _():
-            run([main, local(tiles.at[1], out.at[1], osem.at[1])])
+            run([main])
+            pass_out(1).wait()
 
         sent = t.at[:, pl.ds(0, 576)]
         arrived(sent, s_send)
 
     @pl.when(r >= 11)
     def _():
-        for cp in pass_on():
-            cp.wait()
+        for n in range(2):
+            pass_out(n).wait()
 
     @pl.when(r < 2)
     def _():
@@ -714,8 +803,20 @@
                        osem.at[6 + 4 * k + j]) for k in range(FB) for j in range(FB)]
         run(panel)
 
-    drain_tree(flags_a, a_send, (128, 96, 96))
-    drain_tree(flags_b, b_send, (256, 288, 288))
+    @pl.when(plain)
+    def _():
+        drain_outs(a_out, lambda d: a_send.at[d], 320)
+        drain_outs(b_out, lambda d: b_send.at[d], 832)
+
+        @pl.when((r < 2) & ((y == 1) | (y == 3)))
+        def _():
+            @pl.when(r == 0)
+            def _():
+                drain(y_send.at[0], 160)
+
+            @pl.when(r == 1)
+            def _():
+                drain(y_send.at[1], 416)
 
 
 def on_device(kernel_tiles, profile):
@@ -739,10 +840,10 @@
             pltpu.VMEM((BLK, TILE), BF16),
             pltpu.VMEM((BLK, TILE), BF16),
             dma((12,)), dma((2,)),
-            dma((16,)), dma((16,)), dma((16,)),
-            dma((8,)), dma((8,)), dma((36,)), dma((36,)),
-            dma((3, 4)), dma((3, 4)), dma((3, 4)), dma((3,)),
-            dma((3, 4)), dma((3, 4)), dma, dma((10,)), dma((22,)),
+            dma((32,)), dma((32,)), dma((16,)),
+            dma((32,)), dma((32,)), dma((36,)), dma((36,)),
+            dma((4, 4)), dma((4,)), dma((2, 4)), dma((3, 8)),
+            dma((4,)), dma((4,)), dma((2,)), dma, dma((10,)), dma((22,)),
         ],
         compiler_params=pltpu.CompilerParams(
             vmem_limit_bytes=58 * 2**20, collective_id=0, has_side_effects=True

time: 974 us -> 261 us (0.27)
  the two profiles are of different devices: /device:TPU:11 before, /device:TPU:74 now
where the time goes in v3:
time: 261 us
  Pallas kernels  253 us (97%)
  local copies, waits for them, and re-layouts  8.44 us (3%)
    pallas_call x1, Pallas kernels, on_device(): pl.pallas_call(kernel, out_shape=jax.ShapeDtypeStruct((2, TILE, TILE), F3...  253 us
    unnamed x1, local copies, waits for them, and re-layouts  8.44 us

profile of v3, /device:TPU:74, one launch (start us, length us, event | category | flops | bytes accessed | tf_op | source)
XLA Modules:
  0.0 261.3 jit_solution(3165222107267359872)
XLA Ops:
  0.0 252.8 %panel_steps.1 = f32[2,1024,1024]{2,1,0:T(8,128)} custom-call(f32[2,1024,1024]{2,1,0:T(8,128)} %bitcast.5), custom_call_target="tpu_custom_call" | custom-call | tf_op jit(solution)/shard_map/panel_steps/pallas_call | solution.py:825
  252.8 8.4 %copy.4 = f32[1,1,2,1,1024,1024]{5,4,3,2,1,0:T(8,128)} copy(f32[1,1,2,1,1024,1024]{5,4,3,2,1,0:T(8,128)} %bitcast.4) | data formatting | bytes 16777216

commit v4 on v3

--- a/solution.py
+++ b/solution.py
@@ -116,17 +116,75 @@
 
 
 FB = 4
-SLOTS = 38
-EXTRA_SLOTS = 46
+STREAM_SLOTS = (6, 7, 8, 9, 11, 12, 13, 16, 17, 21)
+SLOT_TIME = 1.5
+PREP, VSUB, VSOLVE, WSUB, WSOLVE, HSUB, HSOLVE, TSUB = range(8)
+
+
+def plan():
+    stream = [STREAM_SLOTS[4 * k - k * (k - 1) // 2] + 8 for k in range(FB)]
+    ops = []
+
+    def add(kind, k, m, ready, after):
+        ops.append(((kind, k, m), ready, after))
+
+    for k in range(FB):
+        add(PREP, k, 0, max(4 * k + 11, stream[k]), [])
+        add(PREP, k, 3, 0, [(HSOLVE, k, 0)])
+        add(PREP, k, 1, 8 * k + 15, [])
+        add(PREP, k, 2, 8 * k + 13, [])
+        add(PREP, FB + k, 0, 2 * k + 15, [])
+    for k in range(FB):
+        for m in range(k):
+            add(WSUB, k, m, 0, [(PREP, k, 0), (WSOLVE, m, 0)])
+            add(HSUB, k, m, 0, [(PREP, k, 0), (HSOLVE, m, 0)])
+            add(VSUB, k, m, 0, [(PREP, k, 0), (PREP, k, 1), (VSOLVE, m, 0)])
+        add(WSOLVE, k, 0, 0, [(PREP, k, 0)] + [(WSUB, k, m) for m in range(k)])
+        add(HSOLVE, k, 0, 0, [(PREP, k, 0)] + [(HSUB, k, m) for m in range(k)])
+        add(VSOLVE, k, 0, 0, [(PREP, k, 0), (PREP, k, 1)] + [(VSUB, k, m) for m in range(k)])
+        add(TSUB, k, 0, 0, [(VSOLVE, k, 0), (WSOLVE, k, 0)])
+    for k in range(FB, NB):
+        for m in range(FB):
+            add(WSUB, k, m, 0, [(PREP, k, 0), (WSOLVE, m, 0), (PREP, m, 3)])
+            add(VSUB, k, m, 0, [(PREP, k - FB, 2), (VSOLVE, m, 0), (PREP, m, 3)])
+    slots, done, slot = [], set(), 0
+    while len(done) < len(ops):
+        here, used = [], 0.0
+        moved = True
+        while moved:
+            moved = False
+            for op, ready, after in ops:
+                cost = {PREP: 0.1, TSUB: 1.8, VSUB: 0.6, VSOLVE: 0.6}.get(op[0], 0.35)
+                fits = used == 0.0 or used + cost <= SLOT_TIME + 0.5
+                if op not in done and ready <= slot and fits and used < SLOT_TIME and all(o in done for o in after):
+                    here.append(op)
+                    done.add(op)
+                    used += cost
+                    moved = True
+                    break
+        slots.append(here)
+        slot += 1
+    return slots
+
+
+def lookup(i, values, other=-1):
+    bits = max(1, (len(values) - 1).bit_length())
+    at = jnp.clip(i, 0, 2 ** bits - 1)
+    level = list(values) + [other] * (2 ** bits - len(values))
+    for b in range(bits):
+        odd = lax.rem(lax.shift_right_logical(at, b), 2) == 1
+        level = [p if isinstance(p, int) and isinstance(q, int) and p == q
+                 else jnp.where(odd, jnp.int32(q), jnp.int32(p)) for p, q in zip(level[::2], level[1::2])]
+    return jnp.where(at == i, level[0], other)
 
 
 def first_id(k):
     return 4 * k - lax.div(k * (k - 1), jnp.int32(2))
 
 
-def kernel(tiles, out, w, v, v10, t, lb, s, work, ph, pw, vh, vw,
-           load, load_t, c_recv, d_recv, e_recv, r_own, r_sib, l_own, l_sib,
-           c_send, d_send, e_send, r_send, a_send, b_send, y_send, s_send, root_send, osem):
+def kernel(tiles, out, w, v, v10, h, t, lb, s, work, ph, pw, vh, vw,
+           load, load_t, c_recv, d_recv, e_recv, h_own, h_full, w_full, p_recv, r_own, r_sib, l_own, l_sib,
+           c_send, d_send, e_send, h_send, w_send, r_send, a_send, b_send, y_send, s_send, root_send, osem):
     r = lax.axis_index("row")
     c = lax.axis_index("col")
     x = lax.div(r, 4)
@@ -167,7 +225,10 @@
 
     y_depth = jnp.where(y == 0, 0, jnp.where(y == 2, 2, 1))
     a_out, a_in, a_depth = stream_tree(0)
-    b_out, b_in, b_depth = stream_tree(1)
+    h_out, b_in, b_depth = stream_tree(1)
+    b_out = (h_out[0], h_out[1] & (x != 2), h_out[2], h_out[3])
+    across = (lax.rem(r + 8, 16), c)
+    odd_x = lax.rem(x, 2) == 1
 
     def remote(src, dst, send, recv, device):
         return pltpu.make_async_remote_copy(
@@ -205,8 +266,15 @@
     def _():
         pl.semaphore_signal(barrier, inc=1, device_id=(1 - r, 1 - c), device_id_type=pl.DeviceIdType.MESH)
 
+    @pl.when(odd_x)
+    def _():
+        pl.semaphore_signal(barrier, inc=1, device_id=across, device_id_type=pl.DeviceIdType.MESH)
+
     def block_cols(n):
         return pl.ds(pl.multiple_of(n * BLK, BLK), BLK)
+
+    half_512 = pl.ds(pl.multiple_of(core * 512, 512), 512)
+    other_512 = pl.ds(pl.multiple_of(512 - core * 512, 512), 512)
 
     def local(src, dst, sem):
         return pltpu.make_async_copy(src, dst, sem)
@@ -226,7 +294,8 @@
         return [local(tiles.at[1, pl.ds(k * BLK, BLK), :], v10.at[k], load.at[8 + k]) for k in range(FB)]
 
     def own_cols():
-        return [local(tiles.at[0, :, pl.ds(k * BLK, BLK)], w.at[4 * core + k], load.at[k]) for k in range(FB)]
+        return [local(tiles.at[0, half_512, pl.ds(k * BLK, BLK)], w.at[4 * core + k, half_512, :], load.at[k])
+                for k in range(FB)]
 
     def target(n):
         return local(tiles.at[slot_a if n == 0 else 1], t.at[n], load_t.at[n])
@@ -257,6 +326,14 @@
         for cp in own_cols():
             cp.start()
 
+    def panel_in():
+        return [local(tiles.at[0, :, pl.ds(k * BLK, BLK)], h.at[k], osem.at[2 + k]) for k in range(FB)]
+
+    @pl.when((r == 1) & (c == 0))
+    def _():
+        for cp in panel_in():
+            cp.start()
+
     @pl.when(r >= 11)
     def _():
         pass_in(0).start()
@@ -266,19 +343,25 @@
     def _():
         pass_in(1).start()
 
-    @pl.when(plain)
+    @pl.when(jnp.logical_not(is_f | is_g | odd_x))
     def _():
         pl.semaphore_wait(barrier, 11)
 
-    @pl.when(is_f | is_g)
+    @pl.when(is_f | is_g | odd_x)
     def _():
         pl.semaphore_wait(barrier, 12)
 
-    @pl.when((full & (y == 0)) | ((r == 1) & (c == 0)))
+    @pl.when(full & (y == 0))
     def _():
         for k in range(FB):
-            remote(tiles.at[0, :, pl.ds(k * BLK, BLK)], w.at[4 * core + k],
+            remote(tiles.at[0, other_512, pl.ds(k * BLK, BLK)], w.at[4 * core + k, other_512, :],
                    r_send.at[2, 4 * core + k], r_sib.at[k], sibling).start()
+
+    @pl.when((r == 1) & (c == 0))
+    def _():
+        for k in range(FB):
+            remote(tiles.at[0, :, pl.ds(k * BLK, BLK)], w.at[k],
+                   r_send.at[2, k], r_sib.at[k], sibling).start()
 
     @pl.when(r == 0)
     def _():
@@ -335,7 +418,7 @@
         def _():
             arrived(ref, d_recv.at[n])
 
-        forward(d_out, ref, lambda d: d_send.at[d], d_recv.at[n])
+        forward(d_out, ref, lambda d: d_send.at[d, k], d_recv.at[n])
 
     def e_ref(n):
         return v10.at[lax.div(n, 4), pl.ds(pl.multiple_of(lax.rem(n, 4) * 64, 64), 64), :]
@@ -358,61 +441,45 @@
 
         forward(c_out[:3] + (c_out[3] | (r == 1),), e_ref(n), lambda d: e_send.at[1, d], e_recv.at[n])
 
-    def r_rows(n, half):
-        return pl.ds(pl.multiple_of(half * 512 + lax.rem(n, 4) * 128, 128), 128)
-
-    def r_event(n):
-        b = lax.div(n, 4)
-        ref = w.at[b, r_rows(n, core), :]
-
+    def r_ref(n):
+        rows = pl.ds(pl.multiple_of(core * 512 + lax.rem(n, 4) * 128, 128), 128)
+        return w.at[lax.div(n, 4), rows, :]
+
+    def r_event(n, way, target, first, last):
         @pl.when(y == 0)
         def _():
-            m = lax.rem(b, 4)
-
-            @pl.when(lax.rem(n, 4) == 0)
-            def _():
-                @pl.when(lax.div(b, 4) == core)
+            if first:
+                b = lax.div(n, 4)
+                m = lax.rem(b, 4)
+
+                @pl.when((lax.rem(n, 4) == 0) & (lax.div(b, 4) == core))
                 def _():
-                    arrived(w.at[b], load.at[m])
-
-                @pl.when(lax.div(b, 4) != core)
+                    arrived(w.at[b, half_512, :], load.at[m])
+
+                @pl.when((lax.rem(n, 4) == 0) & (lax.div(b, 4) != core))
                 def _():
-                    arrived(w.at[b], r_sib.at[m])
-
-            remote(ref, ref, r_send.at[0, b], r_own.at[n], (r, 2 + core)).start()
-            remote(ref, ref, r_send.at[1, b], r_own.at[n], (r, 6 + core)).start()
+                    arrived(w.at[b, half_512, :], r_sib.at[m])
 
         @pl.when(y != 0)
         def _():
-            arrived(ref, r_own.at[n])
-            remote(ref, ref, r_send.at[2, b], r_sib.at[n], sibling).start()
-            odd = lax.rem(n, 2)
-
-            @pl.when(((y == 1) & (odd == 0)) | ((y == 3) & (odd == 1)))
-            def _():
-                remote(ref, ref, r_send.at[0, b], r_own.at[n], (r, 4 + core)).start()
+            arrived(r_ref(n), r_own.at[n])
+
+        @pl.when(y != last)
+        def _():
+            remote(r_ref(n), r_ref(n), r_send.at[way, lax.div(n, 4)], r_own.at[n], (r, target)).start()
 
     def w_ready(b):
-        @pl.when(y == 0)
-        def _():
-            drain(r_send.at[0, b], 128)
-            drain(r_send.at[1, b], 128)
-
-            @pl.when(lax.div(b, 4) == core)
-            def _():
-                drain(r_send.at[2, b], 256)
-
-        @pl.when(y != 0)
+        @pl.when(y != 3)
+        def _():
+            drain(r_send.at[0, b], 64)
+
+        @pl.when(y != 1)
+        def _():
+            drain(r_send.at[1, b], 64)
+
+        @pl.when((y == 0) & (lax.div(b, 4) == core))
         def _():
             drain(r_send.at[2, b], 128)
-
-            @pl.when(y != 2)
-            def _():
-                drain(r_send.at[0, b], 64)
-
-            @pl.loop(4 * b, 4 * b + 4)
-            def _(n):
-                arrived(w.at[b, r_rows(n, 1 - core), :], r_sib.at[n])
 
     half_128 = pl.ds(pl.multiple_of(core * HALF, HALF), HALF)
     other_128 = pl.ds(pl.multiple_of(HALF - core * HALF, HALF), HALF)
@@ -443,8 +510,52 @@
     def b_event(n):
         l_event(n, b_out, b_send, 1)
 
+        @pl.when(x == 3)
+        def _():
+            ref = lb.at[n, half_128, :]
+            remote(ref, ref, y_send.at[3], l_own.at[n], across).start()
+
+    def h_rows(n, half):
+        return pl.ds(pl.multiple_of(half * 512 + lax.rem(n, 4) * 128, 128), 128)
+
+    def h_event(n):
+        k = lax.div(n, 4)
+        ref = h.at[k, h_rows(n, core), :]
+        origin = (r == 1) & (c == 0)
+
+        @pl.when(origin)
+        def _():
+            @pl.when(lax.rem(n, 4) == 0)
+            def _():
+                arrived(h.at[k], osem.at[2 + k])
+
+            for other in (1, 2, 3, 6, 7):
+                part = h.at[k, h_rows(n, other % 2), :]
+                remote(part, part, root_send.at[other], h_own.at[n], (1, other)).start()
+
+        @pl.when(jnp.logical_not(origin))
+        def _():
+            arrived(ref, h_own.at[n])
+
+        forward(h_out, ref, lambda d: h_send.at[d, k], h_own.at[n])
+        odd = lax.rem(n, 2)
+
+        @pl.when((r == 1) & (((y == 1) & (odd == 0)) | ((y == 3) & (odd == 1))))
+        def _():
+            remote(ref, ref, y_send.at[2], h_own.at[n], (r, 4 + core)).start()
+
+    def h_drain(k):
+        drain_outs(h_out, lambda d: h_send.at[d, k], 128)
+
+    def swap(buf, k, send, recv):
+        ref = buf.at[k, half_512, :]
+        remote(ref, ref, send, recv, sibling).start()
+
+    def swapped(buf, k, recv):
+        arrived(buf.at[k, other_512, :], recv)
+
     def last_events(k):
-        lo = 26 + first_id(k)
+        lo = 10 + first_id(k)
 
         @pl.when(b_in)
         def _():
@@ -488,13 +599,10 @@
             remote(ref, ref, root_send.at[other], l_own.at[n], (0, other)).start()
         forward(a_out, lb.at[n, half_of(0), :], lambda d: a_send.at[d], l_own.at[n])
 
-    def send_g(n, both):
+    def send_g(n):
         for other in (0, 2, 3, 6, 7):
             ref = lb.at[n, half_of(other % 2), :]
             remote(ref, ref, root_send.at[other], l_own.at[n], (1, other)).start()
-        if both:
-            ref = lb.at[n, half_of(1), :]
-            remote(ref, ref, root_send.at[8], l_sib.at[n], (1, 0)).start()
         forward(b_out, lb.at[n, half_of(1), :], lambda d: b_send.at[d], l_own.at[n])
 
     def factor_out():
@@ -522,13 +630,17 @@
 
     @pl.when(is_g)
     def _():
+        @pl.loop(0, 32)
+        def _(n):
+            d_event(n)
+
+        @pl.loop(0, 16)
+        def _(n):
+            h_event(n)
+
         for k in range(FB):
             arrived(s.at[k, pl.ds(k * BLK, TILE - k * BLK), :], load.at[4 + k])
             arrived(w.at[k], r_sib.at[k])
-
-        @pl.loop(0, 32)
-        def _(n):
-            d_event(n)
 
         @pl.loop(0, FB)
         def _(k):
@@ -543,8 +655,8 @@
             def _(i):
                 p = dot_nt(w[k, rows_of(i), :], lb[lo])
                 w[k, rows_of(i), :] = p
-                lb[10 + 4 * k + i] = p
-                send_g(10 + 4 * k + i, True)
+                ref = w.at[k, rows_of(i), :]
+                remote(ref, ref, root_send.at[8], p_recv.at[4 * k + i], (1, 0)).start()
 
             @pl.loop(0, FB)
             def _(j):
@@ -558,123 +670,197 @@
                 def _(i):
                     w[j, rows_of(i), :] = w[j, rows_of(i), :] - dot_nt(w[k, rows_of(i), :], lb[lo + j - k])
 
-        chain(26, lambda n: send_g(n, False))
+        chain(10, send_g)
         for cp in factor_out():
             cp.start()
         for cp in factor_out():
             cp.wait()
-        drain_outs(d_out, lambda d: d_send.at[d], 1024)
-        drain_outs(b_out, lambda d: b_send.at[d], 832)
+        for k in range(FB):
+            drain_outs(d_out, lambda d: d_send.at[d, k], 256)
+            h_drain(k)
+        drain_outs(b_out, lambda d: b_send.at[d], 320)
         for other in (0, 2, 3, 6, 7):
-            drain(root_send.at[other], 832)
-        drain(root_send.at[8], 512)
+            drain(root_send.at[other], 320)
+        drain(root_send.at[8], 1024)
 
     def low_id(k, m):
-        return jnp.where(
-            k < 4, first_id(m) + k - m,
-            jnp.where(m < 4, 10 + 4 * m + k - 4, 26 + first_id(m - 4) + k - m),
-        )
-
-    def v_sub(buf, at, k, m):
-        buf[k - at] = buf[k - at] - dot3(split2(lb[low_id(k, m)]), split2(buf[m - at]), 0)
+        return jnp.where(k < FB, first_id(m), 10 + first_id(m - FB)) + k - m
+
+    def v_sub(buf, at, k, low, m):
+        buf[k - at] = buf[k - at] - dot3(split2(low), split2(buf[m - at]), 0)
 
     def v_solve(buf, at, k):
         buf[k - at] = dot3(split2(lb[low_id(k, k)]), split2(buf[k - at]), 0)
-        hi, lo = split2(buf[k - at])
-        vh[...] = hi
-        vw[...] = lo
-
-    def w_sub(k, m):
-        w[k] = w[k] - dot3(split2(w[m]), split2(lb[low_id(k, m)]), 1)
-
-    def w_solve(k):
-        w[k] = dot3(split2(w[k]), split2(lb[low_id(k, k)]), 1)
+
+    def w_sub(buf, k, low, m):
+        buf[k, half_512, :] = buf[k, half_512, :] - dot3(split2(buf[m, half_512, :]), split2(low), 1)
+
+    def w_solve(buf, k, send, recv):
+        buf[k, half_512, :] = dot3(split2(buf[k, half_512, :]), split2(lb[low_id(k, k)]), 1)
+        swap(buf, k, send, recv)
+
+    def t_sub(slot, k, right):
         hi, lo = split2(w[k])
         ph[...] = hi
         pw[...] = lo
-
-    def t_sub(slot):
+        hi, lo = split2(right)
+        vh[...] = hi
+        vw[...] = lo
         for n in range(4):
             cols = pl.ds(n * BLK, BLK)
             t[slot, :, cols] = t[slot, :, cols] - dot3((ph[...], pw[...]), (vh[:, cols], vw[:, cols]), 0)
 
-    def one_row(k, start):
-        @pl.loop(start, k)
+    def late_row(k):
+        @pl.loop(FB, k)
         def _(m):
-            v_sub(v, 0, k, m)
-            w_sub(k, m)
-
+            w_sub(w, k, lb[low_id(k, m)], m)
+            v_sub(v, 0, k, lb[low_id(k, m)], m)
+
+        w_solve(w, k, w_send.at[k], w_full.at[k])
         v_solve(v, 0, k)
-        w_solve(k)
-        t_sub(0)
-
-    def row_of_first(k):
-        w_ready(k)
-        drain_outs(c_out, lambda d: c_send.at[d, k], 256)
-
-        @pl.loop(0, k + 1)
-        def _(m):
-            l_ready(low_id(k, m), 1)
-
-        @pl.when(k == 0)
-        def _():
-            target(0).wait()
-
-        one_row(k, 0)
+        swapped(w, k, w_full.at[k])
+        t_sub(0, k, v[k])
+
+    def run_op(kind, k, m):
+        @pl.when(kind == PREP)
+        def _():
+            @pl.when(m == 0)
+            def _():
+                w_ready(k)
+
+                @pl.when(k < FB)
+                def _():
+                    h_drain(k)
+
+                    @pl.loop(0, k + 1)
+                    def _(q):
+                        l_ready(low_id(k, q), 1)
+
+            @pl.when(m == 1)
+            def _():
+                drain_outs(c_out, lambda d: c_send.at[d, k], 256)
+
+                @pl.when(k == 0)
+                def _():
+                    target(0).wait()
+
+            @pl.when(m == 3)
+            def _():
+                swapped(h, k, h_full.at[k])
+
+            @pl.when(m == 2)
+            def _():
+                drain_outs(d_out, lambda d: d_send.at[d, k], 256)
+
+        @pl.when(kind == VSUB)
+        def _():
+            @pl.when(k < FB)
+            def _():
+                v_sub(v, 0, k, lb[low_id(k, m)], m)
+
+            @pl.when(k >= FB)
+            def _():
+                v_sub(v, 0, k, h[m, rows_of(k - FB), :], m)
+
+        @pl.when(kind == WSUB)
+        def _():
+            @pl.when(k < FB)
+            def _():
+                w_sub(w, k, lb[low_id(k, m)], m)
+
+            @pl.when(k >= FB)
+            def _():
+                w_sub(w, k, h[m, rows_of(k - FB), :], m)
+
+        @pl.when(kind == HSUB)
+        def _():
+            w_sub(h, k, lb[low_id(k, m)], m)
+
+        @pl.when(kind == VSOLVE)
+        def _():
+            v_solve(v, 0, k)
+
+        @pl.when(kind == WSOLVE)
+        def _():
+            w_solve(w, k, w_send.at[k], w_full.at[k])
+
+        @pl.when(kind == HSOLVE)
+        def _():
+            w_solve(h, k, h_send.at[4, k], h_full.at[k])
+
+        @pl.when(kind == TSUB)
+        def _():
+            swapped(w, k, w_full.at[k])
+            t_sub(0, k, v[k])
+
+    table = plan()
+    count = [len(ops) for ops in table]
+    flat = [64 * kind + 8 * k + m for ops in table for kind, k, m in ops]
+    before = [sum(count[:n]) for n in range(len(count))]
 
     @pl.when(plain)
     def _():
-        @pl.loop(0, jnp.where(c == 2, EXTRA_SLOTS, SLOTS))
+        @pl.loop(0, max(len(table), 50))
         def _(slot):
-            n_c = slot - c_depth
+            n_c = slot - 2 * c_depth
 
             @pl.when(c_in & within(n_c, 32))
             def _():
                 c_event(n_c)
 
-            n_d = slot - d_depth
+            n_d = slot - 2 * d_depth
 
             @pl.when(d_in & within(n_d, 32))
             def _():
                 d_event(n_d)
 
-            n_r = slot - y_depth
-
-            @pl.when(full & within(n_r, 32))
-            def _():
-                r_event(n_r)
-
-            n_a = slot - 7 - a_depth - y_depth
-
-            @pl.when(a_in & within(n_a, 20) & (lax.rem(n_a + 16, 2) == 0))
-            def _():
-                a_event(lax.div(n_a, 2))
-
-            n_b = slot - 13 - b_depth - y_depth
-
-            @pl.when(b_in & within(n_b, 16))
-            def _():
-                b_event(10 + n_b)
+            n_r = slot - 2 * y
+
+            @pl.when(full & within(n_r, 16))
+            def _():
+                r_event(2 * n_r, 0, lax.rem(c + 2, 8), True, 3)
+
+            n_s = slot - 2 * lax.rem(4 - y, 4)
+
+            @pl.when(full & within(n_s, 16))
+            def _():
+                r_event(2 * n_s + 1, 1, lax.rem(c + 6, 8), False, 1)
+
+            n_a = lookup(slot - a_depth - y_depth, [STREAM_SLOTS.index(q) if q in STREAM_SLOTS else -1
+                                                      for q in range(STREAM_SLOTS[-1] + 1)])
+
+            @pl.when(a_in & (n_a >= 0))
+            def _():
+                a_event(n_a)
+
+            n_h = slot - b_depth - y_depth
+
+            @pl.when(b_in & within(n_h, 16))
+            def _():
+                h_event(n_h)
 
             @pl.when(c == 2)
             def _():
-                n_e = slot - 32 - d_depth
+                n_e = slot - 32 - 2 * d_depth
 
                 @pl.when(d_in & within(n_e, 8))
                 def _():
                     e_even(n_e)
 
-                n_f = slot - 32 - jnp.where(r == 1, 0, 1 + c_depth)
+                n_f = slot - 32 - jnp.where(r == 1, 0, 2 + 2 * c_depth)
 
                 @pl.when((c_in | (r == 1)) & within(n_f, 8))
                 def _():
                     e_odd(n_f)
 
-            k = jnp.where(slot == 15, 0, jnp.where(slot == 23, 1, jnp.where(slot == 29, 2, jnp.where(slot == 36, 3, -1))))
-
-            @pl.when(full & (k >= 0))
-            def _():
-                row_of_first(k)
+            @pl.when(full)
+            def _():
+                first = lookup(slot, before, 0)
+
+                @pl.loop(first, first + lookup(slot, count, 0))
+                def _(n):
+                    code = lookup(n, flat)
+                    run_op(lax.div(code, 64), lax.rem(lax.div(code, 8), 8), lax.rem(code, 8))
 
     @pl.when(plain & (r < 2))
     def _():
@@ -685,31 +871,34 @@
 
         @pl.when(r == 1)
         def _():
-            drain_outs(d_out, lambda d: d_send.at[d], 1024)
+            for k in range(FB):
+                drain_outs(d_out, lambda d: d_send.at[d, k], 256)
+                h_drain(k)
+
+            @pl.when((y == 1) | (y == 3))
+            def _():
+                drain(y_send.at[2], 256)
+
+            @pl.when(c == 0)
+            def _():
+                for other in (1, 2, 3, 6, 7):
+                    drain(root_send.at[other], 512)
 
     @pl.when(r >= 11)
     def _():
         for k in range(FB):
             drain_outs(c_out, lambda d: c_send.at[d, k], 256)
-        drain_outs(d_out, lambda d: d_send.at[d], 1024)
+            drain_outs(d_out, lambda d: d_send.at[d, k], 256)
+            h_drain(k)
 
     @pl.when(c == 2)
     def _():
         drain_outs(d_out, lambda d: e_send.at[0, d], 512)
         drain_outs(c_out[:3] + (c_out[3] | (r == 1),), lambda d: e_send.at[1, d], 512)
 
-    @pl.when(full)
-    def _():
-        drain_outs(d_out, lambda d: d_send.at[d], 1024)
-        l_ready(10, 16)
-
-        @pl.loop(FB, NB)
-        def _(b):
-            w_ready(b)
-
-        @pl.when(c == 2)
-        def _():
-            target(1).wait()
+    @pl.when(full & (c == 2))
+    def _():
+        target(1).wait()
 
     @pl.when((r == 1) & (c == 0))
     def _():
@@ -718,35 +907,22 @@
 
     @pl.when(plain)
     def _():
-        last_events(0)
-
-        @pl.when(full)
-        def _():
-            @pl.loop(FB, NB)
-            def _(k):
-                @pl.loop(0, FB)
-                def _(m):
-                    v_sub(v, 0, k, m)
-                    w_sub(k, m)
-
         @pl.loop(0, FB)
         def _(k):
-            @pl.when(k > 0)
-            def _():
-                last_events(k)
+            last_events(k)
 
             @pl.when(full)
             def _():
-                one_row(4 + k, 4)
+                late_row(FB + k)
 
                 @pl.when(c == 2)
                 def _():
-                    @pl.loop(4, 4 + k)
+                    @pl.loop(FB, FB + k)
                     def _(m):
-                        v_sub(v10, 4, 4 + k, m)
-
-                    v_solve(v10, 4, 4 + k)
-                    t_sub(1)
+                        v_sub(v10, FB, FB + k, lb[low_id(FB + k, m)], m)
+
+                    v_solve(v10, FB, FB + k)
+                    t_sub(1, FB + k, v10[k])
 
     def run(copies):
         for cp in copies:
@@ -772,8 +948,11 @@
             run([main])
             pass_out(1).wait()
 
-        sent = t.at[:, pl.ds(0, 576)]
-        arrived(sent, s_send)
+        drain(s_send, 640)
+        for k in range(FB):
+            drain(h_send.at[4, k], 128)
+        for k in range(NB):
+            drain(w_send.at[k], 128)
 
     @pl.when(r >= 11)
     def _():
@@ -795,18 +974,19 @@
 
     @pl.when((r == 1) & (c == 0))
     def _():
-        @pl.loop(10, 26)
-        def _(n):
-            arrived(lb.at[n, half_of(1), :], l_sib.at[n])
-
-        panel = [local(lb.at[10 + 4 * k + j], out.at[0, pl.ds(j * BLK, BLK), pl.ds(k * BLK, BLK)],
-                       osem.at[6 + 4 * k + j]) for k in range(FB) for j in range(FB)]
-        run(panel)
+        for k in range(FB):
+            for i in range(FB):
+                arrived(w.at[k, pl.ds(i * BLK, BLK), :], p_recv.at[4 * k + i])
+        run([local(w.at[k], out.at[0, :, pl.ds(k * BLK, BLK)], osem.at[2 + k]) for k in range(FB)])
 
     @pl.when(plain)
     def _():
         drain_outs(a_out, lambda d: a_send.at[d], 320)
-        drain_outs(b_out, lambda d: b_send.at[d], 832)
+        drain_outs(b_out, lambda d: b_send.at[d], 320)
+
+        @pl.when(x == 3)
+        def _():
+            drain(y_send.at[3], 320)
 
         @pl.when((r < 2) & ((y == 1) | (y == 3)))
         def _():
@@ -816,7 +996,7 @@
 
             @pl.when(r == 1)
             def _():
-                drain(y_send.at[1], 416)
+                drain(y_send.at[1], 160)
 
 
 def on_device(kernel_tiles, profile):
@@ -831,8 +1011,9 @@
             pltpu.VMEM((NB, TILE, BLK), F32),
             pltpu.VMEM((NB, BLK, TILE), F32),
             pltpu.VMEM((FB, BLK, TILE), F32),
+            pltpu.VMEM((FB, TILE, BLK), F32),
             pltpu.VMEM((2, TILE, TILE), F32),
-            pltpu.VMEM((36, BLK, BLK), F32),
+            pltpu.VMEM((20, BLK, BLK), F32),
             pltpu.VMEM((FB, TILE, BLK), F32),
             pltpu.VMEM((HALF, 2 * HALF), F32),
             pltpu.VMEM((TILE, BLK), BF16),
@@ -840,10 +1021,10 @@
             pltpu.VMEM((BLK, TILE), BF16),
             pltpu.VMEM((BLK, TILE), BF16),
             dma((12,)), dma((2,)),
-            dma((32,)), dma((32,)), dma((16,)),
-            dma((32,)), dma((32,)), dma((36,)), dma((36,)),
-            dma((4, 4)), dma((4,)), dma((2, 4)), dma((3, 8)),
-            dma((4,)), dma((4,)), dma((2,)), dma, dma((10,)), dma((22,)),
+            dma((32,)), dma((32,)), dma((16,)), dma((16,)), dma((4,)), dma((8,)), dma((16,)),
+            dma((32,)), dma((4,)), dma((20,)), dma((20,)),
+            dma((4, 4)), dma((4, 4)), dma((2, 4)), dma((5, 4)), dma((8,)), dma((3, 8)),
+            dma((4,)), dma((4,)), dma((4,)), dma, dma((10,)), dma((6,)),
         ],
         compiler_params=pltpu.CompilerParams(
             vmem_limit_bytes=58 * 2**20, collective_id=0, has_side_effects=True

time: 261 us -> 228 us (0.87)
  the two profiles are of different devices: /device:TPU:74 before, /device:TPU:76 now
where the time goes in v4:
time: 228 us
  Pallas kernels  220 us (96%)
  local copies, waits for them, and re-layouts  8.44 us (4%)
    pallas_call x1, Pallas kernels, on_device(): pl.pallas_call(kernel, out_shape=jax.ShapeDtypeStruct((2, TILE, TILE), F3...  220 us
    unnamed x1, local copies, waits for them, and re-layouts  8.44 us

profile of v4, /device:TPU:76, one launch (start us, length us, event | category | flops | bytes accessed | tf_op | source)
XLA Modules:
  0.0 228.0 jit_solution(1866443934257213335)
XLA Ops:
  0.0 219.6 %panel_steps.1 = f32[2,1024,1024]{2,1,0:T(8,128)} custom-call(f32[2,1024,1024]{2,1,0:T(8,128)} %bitcast.5), custom_call_target="tpu_custom_call" | custom-call | tf_op jit(solution)/shard_map/panel_steps/pallas_call | solution.py:1005
  219.6 8.4 %copy.4 = f32[1,1,2,1,1024,1024]{5,4,3,2,1,0:T(8,128)} copy(f32[1,1,2,1,1024,1024]{5,4,3,2,1,0:T(8,128)} %bitcast.4) | data formatting | bytes 16777216

commit v5 on v4

--- a/solution.py
+++ b/solution.py
@@ -11,6 +11,7 @@
 HALF = 128
 BLK = 256
 NB = 8
+GROUP = 32
 
 
 def dot_nt(a, b):
@@ -50,37 +51,56 @@
 
 def leaf(work):
     sub = lax.broadcasted_iota(jnp.int32, (8, 2 * HALF), 0)
-    for o in range(0, HALF, 8):
-        rows = [jnp.broadcast_to(work[o + p:o + p + 1, :], (8, 2 * HALF)) for p in range(8)]
-        a = [
-            [jnp.broadcast_to(rows[p][:, o + q:o + q + 1], (8, HALF)) for q in range(p + 1)]
-            for p in range(8)
-        ]
-        low = [[None] * 8 for _ in range(8)]
-        done = []
-        for q in range(8):
-            s = lax.rsqrt(a[q][q])
-            for p in range(q + 1, 8):
-                low[p][q] = a[p][q] * s
-            for p in range(q + 1, 8):
-                for t in range(q + 1, p + 1):
-                    a[p][t] = a[p][t] - low[p][q] * low[t][q]
-            acc = rows[q]
-            for t in range(q):
-                acc = acc - jnp.concatenate([low[q][t], low[q][t]], axis=1) * done[t]
-            done.append(acc * jnp.concatenate([s, s], axis=1))
-        u = done[0]
-        for q in range(1, 8):
-            u = jnp.where(sub == q, done[q], u)
-        work[o:o + 8, :] = u
-        if o + 8 < HALF:
-            h, m, l = split3(u)
+
+    def wide(x):
+        return jnp.concatenate([x, x], axis=1)
+
+    for o in range(0, HALF, GROUP):
+        end = o + GROUP
+        for r in range(o, end, 8):
+            rows = [jnp.broadcast_to(work[r + p:r + p + 1, :], (8, 2 * HALF)) for p in range(8)]
+            a = [
+                [jnp.broadcast_to(rows[p][:, r + q:r + q + 1], (8, HALF)) for q in range(p + 1)]
+                for p in range(8)
+            ]
+            low = [[None] * 8 for _ in range(8)]
+            done = []
+            scale = []
+            for q in range(8):
+                s = lax.rsqrt(a[q][q])
+                scale.append(s)
+                for p in range(q + 1, 8):
+                    low[p][q] = a[p][q] * s
+                for p in range(q + 1, 8):
+                    for t in range(q + 1, p + 1):
+                        a[p][t] = a[p][t] - low[p][q] * low[t][q]
+                acc = rows[q]
+                for t in range(q):
+                    acc = acc - wide(low[q][t]) * done[t]
+                done.append(acc * wide(s))
+            u = done[0]
+            for q in range(1, 8):
+                u = jnp.where(sub == q, done[q], u)
+            work[r:r + 8, :] = u
+            for r2 in range(r + 8, end, 8):
+                x = work[r2:r2 + 8, :]
+                cols = []
+                for q in range(8):
+                    col = jnp.broadcast_to(x[:, r + q:r + q + 1], (8, HALF))
+                    for t in range(q):
+                        col = col - cols[t] * low[q][t]
+                    cols.append(col * scale[q])
+                for q in range(8):
+                    x = x - wide(cols[q]) * done[q]
+                work[r2:r2 + 8, :] = x
+        if end < HALF:
+            h, m, l = split3(work[o:end, :])
             left = jnp.concatenate([v[:, :HALF] for v in (h, h, m, h, l, m)], axis=0).astype(BF16)
             right = jnp.concatenate([h, m, h, l, h, m], axis=0).astype(BF16)
             update = lax.dot_general(
                 left, right, (((0,), (0,)), ((), ())), preferred_element_type=F32
             )
-            work[o + 8:, :] = work[o + 8:, :] - update[o + 8:, :]
+            work[end:, :] = work[end:, :] - update[end:, :]
 
 
 def leaf_factor(work, block):
@@ -116,24 +136,29 @@
 
 
 FB = 4
-STREAM_SLOTS = (6, 7, 8, 9, 11, 12, 13, 16, 17, 21)
+STREAM_SLOTS = (5, 6, 7, 8, 9, 10, 11, 13, 14, 17)
+LAST_SLOTS = (21, 22, 23, 24, 25, 26, 27, 29, 30, 32)
+PANEL_SLOTS = (0, 1, 2, 3, 4, 12, 15, 16, 18, 19, 20, 21, 22, 23, 24, 25)
+EXTRA_SLOT = 32
 SLOT_TIME = 1.5
-PREP, VSUB, VSOLVE, WSUB, WSOLVE, HSUB, HSOLVE, TSUB = range(8)
+PREP, VSUB, VSOLVE, WSUB, WSOLVE, HSUB, HSOLVE, TSUB, XSUB, XSOLVE, XT = range(11)
 
 
 def plan():
-    stream = [STREAM_SLOTS[4 * k - k * (k - 1) // 2] + 8 for k in range(FB)]
+    stream = [q[4 * k - k * (k - 1) // 2] + 8 for q in (STREAM_SLOTS, LAST_SLOTS) for k in range(FB)]
     ops = []
 
     def add(kind, k, m, ready, after):
         ops.append(((kind, k, m), ready, after))
 
     for k in range(FB):
-        add(PREP, k, 0, max(4 * k + 11, stream[k]), [])
+        add(PREP, k, 0, max(PANEL_SLOTS[4 * k + 3] + 8, stream[k]), [])
         add(PREP, k, 3, 0, [(HSOLVE, k, 0)])
         add(PREP, k, 1, 8 * k + 15, [])
         add(PREP, k, 2, 8 * k + 13, [])
         add(PREP, FB + k, 0, 2 * k + 15, [])
+        add(PREP, FB + k, 4, stream[FB + k], [])
+        add(PREP, FB + k, 5, EXTRA_SLOT + 2 * k + 11, [])
     for k in range(FB):
         for m in range(k):
             add(WSUB, k, m, 0, [(PREP, k, 0), (WSOLVE, m, 0)])
@@ -147,6 +172,15 @@
         for m in range(FB):
             add(WSUB, k, m, 0, [(PREP, k, 0), (WSOLVE, m, 0), (PREP, m, 3)])
             add(VSUB, k, m, 0, [(PREP, k - FB, 2), (VSOLVE, m, 0), (PREP, m, 3)])
+        for m in range(FB, k):
+            add(WSUB, k, m, 0, [(PREP, k, 0), (PREP, k, 4), (WSOLVE, m, 0)])
+            add(VSUB, k, m, 0, [(PREP, k - FB, 2), (PREP, k, 4), (VSOLVE, m, 0)])
+            add(XSUB, k, m, 0, [(PREP, k, 4), (PREP, k, 5), (XSOLVE, m, 0)])
+        add(WSOLVE, k, 0, 0, [(PREP, k, 4)] + [(WSUB, k, m) for m in range(k)])
+        add(VSOLVE, k, 0, 0, [(PREP, k, 4)] + [(VSUB, k, m) for m in range(k)])
+        add(XSOLVE, k, 0, 0, [(PREP, k, 4), (PREP, k, 5)] + [(XSUB, k, m) for m in range(FB, k)])
+        add(TSUB, k, 0, 0, [(VSOLVE, k, 0), (WSOLVE, k, 0)])
+        add(XT, k, 0, 0, [(XSOLVE, k, 0), (TSUB, k, 0)])
     slots, done, slot = [], set(), 0
     while len(done) < len(ops):
         here, used = [], 0.0
@@ -154,7 +188,7 @@
         while moved:
             moved = False
             for op, ready, after in ops:
-                cost = {PREP: 0.1, TSUB: 1.8, VSUB: 0.6, VSOLVE: 0.6}.get(op[0], 0.35)
+                cost = {PREP: 0.1, TSUB: 1.8, VSUB: 0.6, VSOLVE: 0.6, XSUB: 0, XSOLVE: 0, XT: 0}.get(op[0], 0.35)
                 fits = used == 0.0 or used + cost <= SLOT_TIME + 0.5
                 if op not in done and ready <= slot and fits and used < SLOT_TIME and all(o in done for o in after):
                     here.append(op)
@@ -226,10 +260,6 @@
     y_depth = jnp.where(y == 0, 0, jnp.where(y == 2, 2, 1))
     a_out, a_in, a_depth = stream_tree(0)
     h_out, b_in, b_depth = stream_tree(1)
-    b_out = (h_out[0], h_out[1] & (x != 2), h_out[2], h_out[3])
-    across = (lax.rem(r + 8, 16), c)
-    odd_x = lax.rem(x, 2) == 1
-
     def remote(src, dst, send, recv, device):
         return pltpu.make_async_remote_copy(
             src_ref=src, dst_ref=dst, send_sem=send, recv_sem=recv,
@@ -266,10 +296,6 @@
     def _():
         pl.semaphore_signal(barrier, inc=1, device_id=(1 - r, 1 - c), device_id_type=pl.DeviceIdType.MESH)
 
-    @pl.when(odd_x)
-    def _():
-        pl.semaphore_signal(barrier, inc=1, device_id=across, device_id_type=pl.DeviceIdType.MESH)
-
     def block_cols(n):
         return pl.ds(pl.multiple_of(n * BLK, BLK), BLK)
 
@@ -343,11 +369,11 @@
     def _():
         pass_in(1).start()
 
-    @pl.when(jnp.logical_not(is_f | is_g | odd_x))
+    @pl.when(plain)
     def _():
         pl.semaphore_wait(barrier, 11)
 
-    @pl.when(is_f | is_g | odd_x)
+    @pl.when(is_f | is_g)
     def _():
         pl.semaphore_wait(barrier, 12)
 
@@ -423,23 +449,18 @@
     def e_ref(n):
         return v10.at[lax.div(n, 4), pl.ds(pl.multiple_of(lax.rem(n, 4) * 64, 64), 64), :]
 
-    def e_even(m):
-        n = 2 * m
-
+    def e_event(n, outs, way):
         @pl.when(r != 1)
         def _():
             arrived(e_ref(n), e_recv.at[n])
 
-        forward(d_out, e_ref(n), lambda d: e_send.at[0, d], e_recv.at[n])
-
-    def e_odd(m):
-        n = 2 * m + 1
-
-        @pl.when(r != 1)
-        def _():
-            arrived(e_ref(n), e_recv.at[n])
-
-        forward(c_out[:3] + (c_out[3] | (r == 1),), e_ref(n), lambda d: e_send.at[1, d], e_recv.at[n])
+        forward(outs, e_ref(n), lambda d: e_send.at[way, d, lax.div(n, 4)], e_recv.at[n])
+
+    e_out = c_out[:3] + (c_out[3] | (r == 1),)
+
+    def e_drain(k):
+        drain_outs(d_out, lambda d: e_send.at[0, d, k], 128)
+        drain_outs(e_out, lambda d: e_send.at[1, d, k], 128)
 
     def r_ref(n):
         rows = pl.ds(pl.multiple_of(core * 512 + lax.rem(n, 4) * 128, 128), 128)
@@ -508,15 +529,14 @@
         l_event(n, a_out, a_send, 0)
 
     def b_event(n):
-        l_event(n, b_out, b_send, 1)
-
-        @pl.when(x == 3)
-        def _():
-            ref = lb.at[n, half_128, :]
-            remote(ref, ref, y_send.at[3], l_own.at[n], across).start()
+        l_event(n, h_out, b_send, 1)
 
     def h_rows(n, half):
         return pl.ds(pl.multiple_of(half * 512 + lax.rem(n, 4) * 128, 128), 128)
+
+    def h_send_to(n, other):
+        part = h.at[lax.div(n, 4), h_rows(n, other % 2), :]
+        remote(part, part, root_send.at[other], h_own.at[n], (1, other)).start()
 
     def h_event(n):
         k = lax.div(n, 4)
@@ -525,13 +545,8 @@
 
         @pl.when(origin)
         def _():
-            @pl.when(lax.rem(n, 4) == 0)
-            def _():
-                arrived(h.at[k], osem.at[2 + k])
-
-            for other in (1, 2, 3, 6, 7):
-                part = h.at[k, h_rows(n, other % 2), :]
-                remote(part, part, root_send.at[other], h_own.at[n], (1, other)).start()
+            for other in (2, 3, 6, 7):
+                h_send_to(n, other)
 
         @pl.when(jnp.logical_not(origin))
         def _():
@@ -553,19 +568,6 @@
 
     def swapped(buf, k, recv):
         arrived(buf.at[k, other_512, :], recv)
-
-    def last_events(k):
-        lo = 10 + first_id(k)
-
-        @pl.when(b_in)
-        def _():
-            @pl.loop(lo, lo + 4 - k)
-            def _(n):
-                b_event(n)
-
-        @pl.when(full)
-        def _():
-            l_ready(lo, 4 - k)
 
     def chain(base, send):
         @pl.loop(0, FB)
@@ -603,7 +605,7 @@
         for other in (0, 2, 3, 6, 7):
             ref = lb.at[n, half_of(other % 2), :]
             remote(ref, ref, root_send.at[other], l_own.at[n], (1, other)).start()
-        forward(b_out, lb.at[n, half_of(1), :], lambda d: b_send.at[d], l_own.at[n])
+        forward(h_out, lb.at[n, half_of(1), :], lambda d: b_send.at[d], l_own.at[n])
 
     def factor_out():
         return [local(s.at[k], out.at[0, :, pl.ds(k * BLK, BLK)], osem.at[2 + k]) for k in range(FB)]
@@ -678,7 +680,7 @@
         for k in range(FB):
             drain_outs(d_out, lambda d: d_send.at[d, k], 256)
             h_drain(k)
-        drain_outs(b_out, lambda d: b_send.at[d], 320)
+        drain_outs(h_out, lambda d: b_send.at[d], 320)
         for other in (0, 2, 3, 6, 7):
             drain(root_send.at[other], 320)
         drain(root_send.at[8], 1024)
@@ -710,17 +712,6 @@
             cols = pl.ds(n * BLK, BLK)
             t[slot, :, cols] = t[slot, :, cols] - dot3((ph[...], pw[...]), (vh[:, cols], vw[:, cols]), 0)
 
-    def late_row(k):
-        @pl.loop(FB, k)
-        def _(m):
-            w_sub(w, k, lb[low_id(k, m)], m)
-            v_sub(v, 0, k, lb[low_id(k, m)], m)
-
-        w_solve(w, k, w_send.at[k], w_full.at[k])
-        v_solve(v, 0, k)
-        swapped(w, k, w_full.at[k])
-        t_sub(0, k, v[k])
-
     def run_op(kind, k, m):
         @pl.when(kind == PREP)
         def _():
@@ -748,27 +739,41 @@
             def _():
                 swapped(h, k, h_full.at[k])
 
+            @pl.when(m == 4)
+            def _():
+                @pl.loop(FB, k + 1)
+                def _(q):
+                    l_ready(low_id(k, q), 1)
+
+            @pl.when((m == 5) & (c == 2))
+            def _():
+                e_drain(k - FB)
+
+                @pl.when(k == FB)
+                def _():
+                    target(1).wait()
+
             @pl.when(m == 2)
             def _():
                 drain_outs(d_out, lambda d: d_send.at[d, k], 256)
 
         @pl.when(kind == VSUB)
         def _():
-            @pl.when(k < FB)
+            @pl.when((k < FB) | (m >= FB))
             def _():
                 v_sub(v, 0, k, lb[low_id(k, m)], m)
 
-            @pl.when(k >= FB)
+            @pl.when((k >= FB) & (m < FB))
             def _():
                 v_sub(v, 0, k, h[m, rows_of(k - FB), :], m)
 
         @pl.when(kind == WSUB)
         def _():
-            @pl.when(k < FB)
+            @pl.when((k < FB) | (m >= FB))
             def _():
                 w_sub(w, k, lb[low_id(k, m)], m)
 
-            @pl.when(k >= FB)
+            @pl.when((k >= FB) & (m < FB))
             def _():
                 w_sub(w, k, h[m, rows_of(k - FB), :], m)
 
@@ -792,15 +797,38 @@
         def _():
             swapped(w, k, w_full.at[k])
             t_sub(0, k, v[k])
+
+        @pl.when(c == 2)
+        def _():
+            @pl.when(kind == XSUB)
+            def _():
+                v_sub(v10, FB, k, lb[low_id(k, m)], m)
+
+            @pl.when(kind == XSOLVE)
+            def _():
+                v_solve(v10, FB, k)
+
+            @pl.when(kind == XT)
+            def _():
+                t_sub(1, k, v10[k - FB])
 
     table = plan()
     count = [len(ops) for ops in table]
     flat = [64 * kind + 8 * k + m for ops in table for kind, k, m in ops]
     before = [sum(count[:n]) for n in range(len(count))]
 
+    @pl.when((r == 1) & (c == 0))
+    def _():
+        for k in range(FB):
+            arrived(h.at[k], osem.at[2 + k])
+
+        @pl.loop(0, 16)
+        def _(n):
+            h_send_to(n, 1)
+
     @pl.when(plain)
     def _():
-        @pl.loop(0, max(len(table), 50))
+        @pl.loop(0, max(len(table), EXTRA_SLOT + 18))
         def _(slot):
             n_c = slot - 2 * c_depth
 
@@ -833,25 +861,33 @@
             def _():
                 a_event(n_a)
 
-            n_h = slot - b_depth - y_depth
-
-            @pl.when(b_in & within(n_h, 16))
+            n_h = lookup(slot - b_depth - y_depth, [PANEL_SLOTS.index(q) if q in PANEL_SLOTS else -1
+                                                    for q in range(PANEL_SLOTS[-1] + 1)])
+
+            @pl.when(b_in & (n_h >= 0))
             def _():
                 h_event(n_h)
 
+            n_b = lookup(slot - b_depth - y_depth, [LAST_SLOTS.index(q) if q in LAST_SLOTS else -1
+                                                    for q in range(LAST_SLOTS[-1] + 1)])
+
+            @pl.when(b_in & (n_b >= 0))
+            def _():
+                b_event(10 + n_b)
+
             @pl.when(c == 2)
             def _():
-                n_e = slot - 32 - 2 * d_depth
+                n_e = slot - EXTRA_SLOT - 2 * d_depth
 
                 @pl.when(d_in & within(n_e, 8))
                 def _():
-                    e_even(n_e)
-
-                n_f = slot - 32 - jnp.where(r == 1, 0, 2 + 2 * c_depth)
+                    e_event(2 * n_e, d_out, 0)
+
+                n_f = slot - EXTRA_SLOT - jnp.where(r == 1, 0, 2 + 2 * c_depth)
 
                 @pl.when((c_in | (r == 1)) & within(n_f, 8))
                 def _():
-                    e_odd(n_f)
+                    e_event(2 * n_f + 1, e_out, 1)
 
             @pl.when(full)
             def _():
@@ -891,38 +927,15 @@
             drain_outs(d_out, lambda d: d_send.at[d, k], 256)
             h_drain(k)
 
-    @pl.when(c == 2)
-    def _():
-        drain_outs(d_out, lambda d: e_send.at[0, d], 512)
-        drain_outs(c_out[:3] + (c_out[3] | (r == 1),), lambda d: e_send.at[1, d], 512)
-
-    @pl.when(full & (c == 2))
-    def _():
-        target(1).wait()
+    @pl.when((c == 2) & jnp.logical_not(full))
+    def _():
+        for k in range(FB):
+            e_drain(k)
 
     @pl.when((r == 1) & (c == 0))
     def _():
         for k in range(FB):
             drain(r_send.at[2, k], 256)
-
-    @pl.when(plain)
-    def _():
-        @pl.loop(0, FB)
-        def _(k):
-            last_events(k)
-
-            @pl.when(full)
-            def _():
-                late_row(FB + k)
-
-                @pl.when(c == 2)
-                def _():
-                    @pl.loop(FB, FB + k)
-                    def _(m):
-                        v_sub(v10, FB, FB + k, lb[low_id(FB + k, m)], m)
-
-                    v_solve(v10, FB, FB + k)
-                    t_sub(1, FB + k, v10[k])
 
     def run(copies):
         for cp in copies:
@@ -982,11 +995,7 @@
     @pl.when(plain)
     def _():
         drain_outs(a_out, lambda d: a_send.at[d], 320)
-        drain_outs(b_out, lambda d: b_send.at[d], 320)
-
-        @pl.when(x == 3)
-        def _():
-            drain(y_send.at[3], 320)
+        drain_outs(h_out, lambda d: b_send.at[d], 320)
 
         @pl.when((r < 2) & ((y == 1) | (y == 3)))
         def _():
@@ -1023,8 +1032,8 @@
             dma((12,)), dma((2,)),
             dma((32,)), dma((32,)), dma((16,)), dma((16,)), dma((4,)), dma((8,)), dma((16,)),
             dma((32,)), dma((4,)), dma((20,)), dma((20,)),
-            dma((4, 4)), dma((4, 4)), dma((2, 4)), dma((5, 4)), dma((8,)), dma((3, 8)),
-            dma((4,)), dma((4,)), dma((4,)), dma, dma((10,)), dma((6,)),
+            dma((4, 4)), dma((4, 4)), dma((2, 4, 4)), dma((5, 4)), dma((8,)), dma((3, 8)),
+            dma((4,)), dma((4,)), dma((3,)), dma, dma((10,)), dma((6,)),
         ],
         compiler_params=pltpu.CompilerParams(
             vmem_limit_bytes=58 * 2**20, collective_id=0, has_side_effects=True

time: 228 us -> 214 us (0.939); the launches traced: 228 us -> 212 us
  Pallas kernels: 220 us -> 203 us
    pallas_call x1, Pallas kernels: 220 us -> 203 us  [on_device(): pl.pallas_call(kernel, out_shape=jax.ShapeDtypeStruct((2, TILE, TILE), F3...]
where the time goes in v5:
time: 214 us; the launch traced here: 212 us
  Pallas kernels  203 us (95%)
  local copies, waits for them, and re-layouts  8.44 us (4%)
    pallas_call x1, Pallas kernels, on_device(): pl.pallas_call(kernel, out_shape=jax.ShapeDtypeStruct((2, TILE, TILE), F3...  203 us
    unnamed x1, local copies, waits for them, and re-layouts  8.44 us

profile of v5, /device:TPU:76, one launch (start us, length us, event | category | flops | bytes accessed | tf_op | source)
XLA Modules:
  0.0 211.5 jit_solution(18307379404348029655)
XLA Ops:
  0.0 203.1 %panel_steps.1 = f32[2,1024,1024]{2,1,0:T(8,128)} custom-call(f32[2,1024,1024]{2,1,0:T(8,128)} %bitcast.5), custom_call_target="tpu_custom_call" | custom-call | tf_op jit(solution)/shard_map/panel_steps/pallas_call | solution.py:1014
  203.1 8.4 %copy.4 = f32[1,1,2,1,1024,1024]{5,4,3,2,1,0:T(8,128)} copy(f32[1,1,2,1,1024,1024]{5,4,3,2,1,0:T(8,128)} %bitcast.4) | data formatting | bytes 16777216

commit v6 on v5

--- a/solution.py
+++ b/solution.py
@@ -152,7 +152,8 @@
         ops.append(((kind, k, m), ready, after))
 
     for k in range(FB):
-        add(PREP, k, 0, max(PANEL_SLOTS[4 * k + 3] + 8, stream[k]), [])
+        add(PREP, k, 0, max(2 * k + 9, stream[k]), [])
+        add(PREP, k, 6, PANEL_SLOTS[4 * k + 3] + 8, [])
         add(PREP, k, 3, 0, [(HSOLVE, k, 0)])
         add(PREP, k, 1, 8 * k + 15, [])
         add(PREP, k, 2, 8 * k + 13, [])
@@ -162,10 +163,10 @@
     for k in range(FB):
         for m in range(k):
             add(WSUB, k, m, 0, [(PREP, k, 0), (WSOLVE, m, 0)])
-            add(HSUB, k, m, 0, [(PREP, k, 0), (HSOLVE, m, 0)])
+            add(HSUB, k, m, 0, [(PREP, k, 0), (PREP, k, 6), (HSOLVE, m, 0)])
             add(VSUB, k, m, 0, [(PREP, k, 0), (PREP, k, 1), (VSOLVE, m, 0)])
         add(WSOLVE, k, 0, 0, [(PREP, k, 0)] + [(WSUB, k, m) for m in range(k)])
-        add(HSOLVE, k, 0, 0, [(PREP, k, 0)] + [(HSUB, k, m) for m in range(k)])
+        add(HSOLVE, k, 0, 0, [(PREP, k, 0), (PREP, k, 6)] + [(HSUB, k, m) for m in range(k)])
         add(VSOLVE, k, 0, 0, [(PREP, k, 0), (PREP, k, 1)] + [(VSUB, k, m) for m in range(k)])
         add(TSUB, k, 0, 0, [(VSOLVE, k, 0), (WSOLVE, k, 0)])
     for k in range(FB, NB):
@@ -178,7 +179,8 @@
             add(XSUB, k, m, 0, [(PREP, k, 4), (PREP, k, 5), (XSOLVE, m, 0)])
         add(WSOLVE, k, 0, 0, [(PREP, k, 4)] + [(WSUB, k, m) for m in range(k)])
         add(VSOLVE, k, 0, 0, [(PREP, k, 4)] + [(VSUB, k, m) for m in range(k)])
-        add(XSOLVE, k, 0, 0, [(PREP, k, 4), (PREP, k, 5)] + [(XSUB, k, m) for m in range(FB, k)])
+        add(XSOLVE, k, 0, 0, [(PREP, k, 4), (PREP, k, 5)] + [(XSUB, k, m) for m in range(FB, k)]
+            + [(XT, m, 0) for m in range(FB, k)])
         add(TSUB, k, 0, 0, [(VSOLVE, k, 0), (WSOLVE, k, 0)])
         add(XT, k, 0, 0, [(XSOLVE, k, 0), (TSUB, k, 0)])
     slots, done, slot = [], set(), 0
@@ -216,7 +218,7 @@
     return 4 * k - lax.div(k * (k - 1), jnp.int32(2))
 
 
-def kernel(tiles, out, w, v, v10, h, t, lb, s, work, ph, pw, vh, vw,
+def kernel(tiles, out, w, v, v10, h, t, lb, s, work, ph, pw, vh, vw, xh, xw,
            load, load_t, c_recv, d_recv, e_recv, h_own, h_full, w_full, p_recv, r_own, r_sib, l_own, l_sib,
            c_send, d_send, e_send, h_send, w_send, r_send, a_send, b_send, y_send, s_send, root_send, osem):
     r = lax.axis_index("row")
@@ -389,20 +391,10 @@
             remote(tiles.at[0, :, pl.ds(k * BLK, BLK)], w.at[k],
                    r_send.at[2, k], r_sib.at[k], sibling).start()
 
-    @pl.when(r == 0)
-    def _():
-        for cp in tile_rows(0):
+    @pl.when((r == 1) & (c == 2))
+    def _():
+        for cp in extra_rows():
             cp.wait()
-
-    @pl.when(r == 1)
-    def _():
-        for cp in tile_rows(4):
-            cp.wait()
-
-        @pl.when(c == 2)
-        def _():
-            for cp in extra_rows():
-                cp.wait()
 
     @pl.when(r >= 11)
     def _():
@@ -434,6 +426,10 @@
         def _():
             arrived(ref, c_recv.at[n])
 
+        @pl.when((r == 0) & (lax.rem(n, 8) == 0))
+        def _():
+            arrived(v.at[k], load.at[k])
+
         forward(c_out, ref, lambda d: c_send.at[d, k], c_recv.at[n])
 
     def d_event(n):
@@ -443,6 +439,10 @@
         @pl.when(r != 1)
         def _():
             arrived(ref, d_recv.at[n])
+
+        @pl.when((r == 1) & (lax.rem(n, 8) == 0))
+        def _():
+            arrived(v.at[4 + k], load.at[k])
 
         forward(d_out, ref, lambda d: d_send.at[d, k], d_recv.at[n])
 
@@ -688,11 +688,23 @@
     def low_id(k, m):
         return jnp.where(k < FB, first_id(m), 10 + first_id(m - FB)) + k - m
 
-    def v_sub(buf, at, k, low, m):
-        buf[k - at] = buf[k - at] - dot3(split2(low), split2(buf[m - at]), 0)
-
-    def v_solve(buf, at, k):
-        buf[k - at] = dot3(split2(lb[low_id(k, k)]), split2(buf[k - at]), 0)
+    def v_sub(k, low, m):
+        v[k] = v[k] - dot3(split2(low), (vh[m], vw[m]), 0)
+
+    def v_solve(k):
+        solved = dot3(split2(lb[low_id(k, k)]), split2(v[k]), 0)
+        hi, lo = split2(solved)
+        vh[k] = hi
+        vw[k] = lo
+
+    def x_sub(k, m):
+        v10[k - FB] = v10[k - FB] - dot3(split2(lb[low_id(k, m)]), split2(v10[m - FB]), 0)
+
+    def x_solve(k):
+        v10[k - FB] = dot3(split2(lb[low_id(k, k)]), split2(v10[k - FB]), 0)
+        hi, lo = split2(v10[k - FB])
+        xh[...] = hi
+        xw[...] = lo
 
     def w_sub(buf, k, low, m):
         buf[k, half_512, :] = buf[k, half_512, :] - dot3(split2(buf[m, half_512, :]), split2(low), 1)
@@ -705,12 +717,11 @@
         hi, lo = split2(w[k])
         ph[...] = hi
         pw[...] = lo
-        hi, lo = split2(right)
-        vh[...] = hi
-        vw[...] = lo
         for n in range(4):
             cols = pl.ds(n * BLK, BLK)
-            t[slot, :, cols] = t[slot, :, cols] - dot3((ph[...], pw[...]), (vh[:, cols], vw[:, cols]), 0)
+            t[slot, :, cols] = t[slot, :, cols] - dot3(
+                (ph[...], pw[...]), (right[0][:, cols], right[1][:, cols]), 0
+            )
 
     def run_op(kind, k, m):
         @pl.when(kind == PREP)
@@ -721,8 +732,6 @@
 
                 @pl.when(k < FB)
                 def _():
-                    h_drain(k)
-
                     @pl.loop(0, k + 1)
                     def _(q):
                         l_ready(low_id(k, q), 1)
@@ -739,6 +748,10 @@
             def _():
                 swapped(h, k, h_full.at[k])
 
+            @pl.when(m == 6)
+            def _():
+                h_drain(k)
+
             @pl.when(m == 4)
             def _():
                 @pl.loop(FB, k + 1)
@@ -761,11 +774,11 @@
         def _():
             @pl.when((k < FB) | (m >= FB))
             def _():
-                v_sub(v, 0, k, lb[low_id(k, m)], m)
+                v_sub(k, lb[low_id(k, m)], m)
 
             @pl.when((k >= FB) & (m < FB))
             def _():
-                v_sub(v, 0, k, h[m, rows_of(k - FB), :], m)
+                v_sub(k, h[m, rows_of(k - FB), :], m)
 
         @pl.when(kind == WSUB)
         def _():
@@ -783,7 +796,7 @@
 
         @pl.when(kind == VSOLVE)
         def _():
-            v_solve(v, 0, k)
+            v_solve(k)
 
         @pl.when(kind == WSOLVE)
         def _():
@@ -796,21 +809,21 @@
         @pl.when(kind == TSUB)
         def _():
             swapped(w, k, w_full.at[k])
-            t_sub(0, k, v[k])
+            t_sub(0, k, (vh.at[k], vw.at[k]))
 
         @pl.when(c == 2)
         def _():
             @pl.when(kind == XSUB)
             def _():
-                v_sub(v10, FB, k, lb[low_id(k, m)], m)
+                x_sub(k, m)
 
             @pl.when(kind == XSOLVE)
             def _():
-                v_solve(v10, FB, k)
+                x_solve(k)
 
             @pl.when(kind == XT)
             def _():
-                t_sub(1, k, v10[k - FB])
+                t_sub(1, k, (xh, xw))
 
     table = plan()
     count = [len(ops) for ops in table]
@@ -1006,6 +1019,21 @@
             @pl.when(r == 1)
             def _():
                 drain(y_send.at[1], 160)
+
+
+def hand_on(src, out, buf, load, store):
+    def parts(n):
+        return n // 4, pl.ds(n % 4 * BLK, BLK)
+
+    loads = [pltpu.make_async_copy(src.at[parts(n)], buf.at[parts(n)], load.at[n]) for n in range(8)]
+    stores = [pltpu.make_async_copy(buf.at[parts(n)], out.at[parts(n)], store.at[n]) for n in range(8)]
+    for cp in loads:
+        cp.start()
+    for n in range(8):
+        loads[n].wait()
+        stores[n].start()
+    for cp in stores:
+        cp.wait()
 
 
 def on_device(kernel_tiles, profile):
@@ -1027,6 +1055,8 @@
             pltpu.VMEM((HALF, 2 * HALF), F32),
             pltpu.VMEM((TILE, BLK), BF16),
             pltpu.VMEM((TILE, BLK), BF16),
+            pltpu.VMEM((NB, BLK, TILE), BF16),
+            pltpu.VMEM((NB, BLK, TILE), BF16),
             pltpu.VMEM((BLK, TILE), BF16),
             pltpu.VMEM((BLK, TILE), BF16),
             dma((12,)), dma((2,)),
@@ -1040,6 +1070,15 @@
         ),
         name="panel_steps",
     )(tiles)
+    out = pl.pallas_call(
+        hand_on,
+        out_shape=jax.ShapeDtypeStruct((2, TILE, TILE), F32),
+        in_specs=[pl.BlockSpec(memory_space=pl.ANY)],
+        out_specs=pl.BlockSpec(memory_space=pl.ANY),
+        scratch_shapes=[pltpu.VMEM((2, TILE, TILE), F32), dma((8,)), dma((8,))],
+        compiler_params=pltpu.CompilerParams(vmem_limit_bytes=56 * 2**20),
+        name="hand_on",
+    )(out)
     return out.reshape(kernel_tiles.shape)
 
 

time: 214 us -> 211 us (0.986)
  local copies, waits for them, and re-layouts: 8.44 us -> 0 us
  Pallas kernels: 203 us -> 208 us
    unnamed x1 -> x0, local copies, waits for them, and re-layouts: 8.44 us -> none
    pallas_call x0 -> x1, Pallas kernels: none -> 6.42 us  [on_device(): pl.pallas_call(hand_on, out_shape=jax.ShapeDtypeStruct((2, TILE, TILE), F...]
where the time goes in v6:
time: 211 us; the launch traced here: 208 us
  Pallas kernels  208 us (99%)
    pallas_call x1, Pallas kernels, on_device(): pl.pallas_call(kernel, out_shape=jax.ShapeDtypeStruct((2, TILE, TILE), F3...  202 us
    pallas_call x1, Pallas kernels, on_device(): pl.pallas_call(hand_on, out_shape=jax.ShapeDtypeStruct((2, TILE, TILE), F...  6.42 us

profile of v6, /device:TPU:76, one launch (start us, length us, event | category | flops | bytes accessed | tf_op | source)
XLA Modules:
  0.0 208.4 jit_solution(6928541422010167466)
XLA Ops:
  0.0 201.8 %panel_steps.1.src = f32[2,1024,1024]{2,1,0:T(8,128)} custom-call(f32[2,1024,1024]{2,1,0:T(8,128)} %bitcast.4), custom_call_target="tpu_custom_call" | custom-call | tf_op jit(solution)/shard_map/panel_steps/pallas_call | solution.py:1042
  201.8 6.4 %hand_on.1 = f32[2,1024,1024]{2,1,0:T(8,128)} custom-call(f32[2,1024,1024]{2,1,0:T(8,128)} %panel_steps.1.src), custom_call_target="tpu_custom_call" | custom-call | tf_op jit(solution)/shard_map/hand_on/pallas_call | solution.py:1073

commit v7 on v6

--- a/solution.py
+++ b/solution.py
@@ -139,7 +139,7 @@
 STREAM_SLOTS = (5, 6, 7, 8, 9, 10, 11, 13, 14, 17)
 LAST_SLOTS = (21, 22, 23, 24, 25, 26, 27, 29, 30, 32)
 PANEL_SLOTS = (0, 1, 2, 3, 4, 12, 15, 16, 18, 19, 20, 21, 22, 23, 24, 25)
-EXTRA_SLOT = 32
+EXTRA_SLOT = 26
 SLOT_TIME = 1.5
 PREP, VSUB, VSOLVE, WSUB, WSOLVE, HSUB, HSOLVE, TSUB, XSUB, XSOLVE, XT = range(11)
 

time: 211 us -> 219 us (1.038); the launches traced: 208 us -> 219 us
  Pallas kernels: 208 us -> 219 us
    pallas_call x1, Pallas kernels: 202 us -> 213 us  [on_device(): pl.pallas_call(kernel, out_shape=jax.ShapeDtypeStruct((2, TILE, TILE), F3...]
where the time goes in v7:
time: 219 us
  Pallas kernels  219 us (100%)
    pallas_call x1, Pallas kernels, on_device(): pl.pallas_call(kernel, out_shape=jax.ShapeDtypeStruct((2, TILE, TILE), F3...  213 us
    pallas_call x1, Pallas kernels, on_device(): pl.pallas_call(hand_on, out_shape=jax.ShapeDtypeStruct((2, TILE, TILE), F...  6.42 us

profile of v7, /device:TPU:76, one launch (start us, length us, event | category | flops | bytes accessed | tf_op | source)
XLA Modules:
  0.0 219.4 jit_solution(15992220255685630846)
XLA Ops:
  0.0 212.8 %panel_steps.1.src = f32[2,1024,1024]{2,1,0:T(8,128)} custom-call(f32[2,1024,1024]{2,1,0:T(8,128)} %bitcast.4), custom_call_target="tpu_custom_call" | custom-call | tf_op jit(solution)/shard_map/panel_steps/pallas_call | solution.py:1042
  212.8 6.4 %hand_on.1 = f32[2,1024,1024]{2,1,0:T(8,128)} custom-call(f32[2,1024,1024]{2,1,0:T(8,128)} %panel_steps.1.src), custom_call_target="tpu_custom_call" | custom-call | tf_op jit(solution)/shard_map/hand_on/pallas_call | solution.py:1073
